TPU v7x, 32 devices: a whole 2x2x4 slice. The times are simulated.
32 devices in a mesh: dp: 4 (over y, x), mp: 8 (over z, core).
Axes of the slice: x: 2, y: 2, z: 4, core: 2. Of those that a mesh axis runs over, the one named last changes fastest.
Arguments:
- activations: bfloat16 [2048, 4096], P('dp', 'mp'), may hold values from -22 to 22
- out_grads: bfloat16 [2048, 32768], P('dp', 'mp'), may hold values from -1 to 1
- weight: float32 [4096, 32768], P('dp', 'mp'), may hold values from -0.09375 to 0.09375
- row_state: float32 [4096], P('dp'), may hold values from 0.1 to 1.6
- column_state: float32 [32768], P('mp'), may hold values from 0.1 to 1.6
- next_batch: bfloat16 [2048, 4096], P('dp', 'mp'), may hold values from -6 to 6
Outputs:
- new_weight: float32 [4096, 32768], P('dp', 'mp')
- update: float32 [4096, 32768], P('dp', 'mp')
- row_moment: float32 [4096], P('dp')
- column_moment: float32 [32768], P('mp')
- next_hidden: bfloat16 [2048, 32768], P('dp', 'mp')
All inputs are finite; a program needn't handle non-finite values.
Results may differ from a plain program's by a relative error of at most 0.001.
The roundings to bfloat16 on the way count: a program that leaves them out, or rounds other values in their place, can miss the bound.
Values may be sent and summed in bfloat16 or wider, within the bound.
No kernel may reach another device: no remote copies, remote signals or barrier semaphores. Data moves between devices by JAX's collectives and lax.ppermute only.
A program may use at most 192 MiB of HBM per device.

v0:
```python
import functools

import jax
import jax.numpy as jnp
from jax import lax
from jax.experimental import pallas as pl
from jax.experimental.pallas import tpu as pltpu
from jax.sharding import PartitionSpec as P

tiny_square = 1e-30
weight_eps = 1e-06
decay_rate = 0.5
clip_level = 0.5
learn_rate = 0.01

f32, bf16 = jnp.float32, jnp.bfloat16
LANES = 128
GRADIENT_SHARES = (3, 3, 3, 3, 2, 2)
UPDATE_SHARES = (1, 1, 2, 2, 3, 3, 2, 2)
SCALE_ROWS = 16
VMEM = 36 * 2**20
SPAN, BASE = 252.0, 125.5


def swap(value, axis, size, bits):
    return lax.ppermute(value, axis, [(i, i ^ bits) for i in range(size)])


def all_sum(value, axis, size):
    bit = 1
    while bit < size:
        pair = value + swap(value, axis, size, bit)
        if 2 * bit < size:
            pair = pair + (swap(value, axis, size, 2 * bit) + swap(value, axis, size, 3 * bit))
        value = pair
        bit *= 4
    return value


def bit_order(dp, chunk):
    bits = [1 << n for n in range(dp.bit_length() - 1)]
    turn = chunk % len(bits)
    return bits[turn:] + bits[:turn]


def cost(flops, bytes_accessed, transcendentals, share=0.01):
    return pl.CostEstimate(
        flops=int(flops * share),
        bytes_accessed=int(bytes_accessed * share),
        transcendentals=int(transcendentals * share),
    )


def params():
    return pltpu.CompilerParams(vmem_limit_bytes=VMEM)


def encode(values):
    top = jnp.max(jnp.abs(values), axis=0, keepdims=True)
    top = jnp.maximum(top * 1.01, 1e-30).astype(bf16)
    part = jnp.sqrt(jnp.abs(values) * (1.0 / top.astype(f32)))
    size = jnp.exp2(part * SPAN - BASE)
    return jnp.where(values < 0, -size, size).astype(bf16), top


def decode(code, top):
    code = code.astype(f32)
    part = (jnp.log2(jnp.abs(code)) + BASE) * (1.0 / SPAN)
    size = part * part * top.astype(f32)
    return jnp.where(code < 0, -size, size)


def put_code(out_ref, code, top):
    rows = code.shape[0]
    out_ref[0:rows, :] = code
    out_ref[rows : rows + SCALE_ROWS, :] = jnp.broadcast_to(top, (SCALE_ROWS, top.shape[1]))


def get_code(ref):
    rows = ref.shape[0] - SCALE_ROWS
    return decode(ref[0:rows, :], ref[rows : rows + 1, :])


def gradient_kernel(dp, first, *refs):
    left = refs[0]
    blocks = refs[1 : 1 + dp]
    gradient, rows, columns = refs[-3:]
    tokens = jnp.concatenate([block[...] for block in blocks], axis=0)
    total = []
    for i in range(left.shape[1]):
        pieces = [left[o, i, n] for n in range(dp) for o in range(dp)]
        total.append(jnp.dot(jnp.concatenate(pieces, axis=1), tokens, preferred_element_type=f32))
    total = jnp.concatenate(total, axis=0)
    gradient[...] = total
    squares = total * total + tiny_square
    columns[...] = jnp.sum(squares, axis=0, keepdims=True)
    lanes = squares[:, 0:LANES]
    for n in range(1, squares.shape[1] // LANES):
        lanes = lanes + squares[:, n * LANES : (n + 1) * LANES]

    @pl.when(pl.program_id(0) == 0)
    def _():
        rows[...] = lanes if first else refs[1 + dp][...] + lanes

    @pl.when(pl.program_id(0) > 0)
    def _():
        rows[...] += lanes


def gradient_chunk(left, own, near, far, before, start, offset, width):
    dp, inner, _, width_of_part, _ = left.shape
    depth, columns = own.shape
    rows, tokens = inner * width_of_part, dp * depth
    tile = tile_of(start, width)
    at = start // tile
    whole = lambda shape: pl.BlockSpec(shape, lambda j: (0, 0))
    inside = pl.BlockSpec((depth, tile), lambda j: (0, at + j))
    apart = pl.BlockSpec((depth, tile), lambda j: (0, j))
    shifted = pl.BlockSpec((depth, tile), lambda j: (0, (start - offset) // tile + j))
    in_specs = [pl.BlockSpec(memory_space=pltpu.VMEM), inside]
    args = [left, own]
    for n in range(1, dp):
        args.append(near[n] if n in near else far[n])
        in_specs.append(shifted if n in near else apart)
    aliases = {}
    if before is not None:
        gradient, row_part, column_part = before
        aliases = {len(args) + 1: 0, len(args) + 2: 2}
        args += [row_part, gradient, column_part]
        in_specs += [whole((rows, LANES)), pl.BlockSpec(memory_space=pl.ANY), pl.BlockSpec(memory_space=pl.ANY)]
    return pl.pallas_call(
        functools.partial(gradient_kernel, dp, before is None),
        grid=(width // tile,),
        in_specs=in_specs,
        out_specs=[
            pl.BlockSpec((rows, tile), lambda j: (0, at + j)),
            whole((rows, LANES)),
            pl.BlockSpec((1, tile), lambda j: (0, at + j)),
        ],
        out_shape=[
            jax.ShapeDtypeStruct((rows, columns), f32),
            jax.ShapeDtypeStruct((rows, LANES), f32),
            jax.ShapeDtypeStruct((1, columns), f32),
        ],
        input_output_aliases=aliases,
        compiler_params=params(),
        cost_estimate=cost(
            flops=2 * rows * tokens * width, bytes_accessed=4 * rows * width + 2 * tokens * (rows + width), transcendentals=0
        ),
        name="gradient_chunk",
    )(*args)


def update_kernel(orders, steps, step, gradient, weight, row_scale, column_scale, features, *refs):
    members = len(orders)
    new_weight, update = refs[-2 - 2 * members : -2 * members]
    sent, kept = refs[-2 * members : -members], refs[-members:]
    change = gradient[...] * row_scale[...] * column_scale[...]
    update[...] = change
    fresh = weight[...] - step[0, 0] * change
    new_weight[...] = fresh
    half = fresh.astype(bf16)
    member = pl.program_id(0) // steps
    parts = []
    for place in range(len(orders[0])):
        n = orders[0][place]
        for g in range(1, members):
            n = jnp.where(member == g, orders[g][place], n)
        pieces = [features[:, i, n].reshape(-1, features.shape[-1]) for i in range(features.shape[1])]
        parts.append(jnp.dot(jnp.concatenate(pieces, axis=1), half, preferred_element_type=f32))
    middle = len(parts) // 2
    stay = jnp.concatenate(parts[:middle], axis=0)
    code, top = encode(jnp.concatenate(parts[middle:], axis=0))
    for g in range(members):

        @pl.when(member == g)
        def _():
            kept[g][...] = stay
            put_code(sent[g], code, top)


def update_chunks(gradient, weight, row_scale, column_scale, step, features, before, start, width, orders):
    rows, columns = gradient.shape
    depth = features.shape[0] * features.shape[3]
    tokens = depth * len(orders[0])
    tile = tile_of(start, width)
    at, steps, members = start // tile, width // tile, len(orders)
    block = pl.BlockSpec((rows, tile), lambda j: (0, at + j))
    own = lambda height, g: pl.BlockSpec((height, tile), lambda j: (0, jnp.clip(j - g * steps, 0, steps - 1)))
    args = [step, gradient, weight, row_scale, column_scale, features]
    in_specs = [
        pl.BlockSpec(memory_space=pltpu.SMEM),
        block,
        block,
        pl.BlockSpec((rows, 1), lambda j: (0, 0)),
        pl.BlockSpec((1, tile), lambda j: (0, at + j)),
        pl.BlockSpec(memory_space=pltpu.VMEM),
    ]
    aliases = {}
    if before is not None:
        aliases = {len(args): 0, len(args) + 1: 1}
        args += list(before)
        in_specs += [pl.BlockSpec(memory_space=pl.ANY)] * 2
    half = tokens // 2
    out = pl.pallas_call(
        functools.partial(update_kernel, orders, steps),
        grid=(members * steps,),
        in_specs=in_specs,
        out_specs=[block, block]
        + [own(half + SCALE_ROWS, g) for g in range(members)]
        + [own(half, g) for g in range(members)],
        out_shape=[jax.ShapeDtypeStruct((rows, columns), f32)] * 2
        + [jax.ShapeDtypeStruct((half + SCALE_ROWS, width), bf16)] * members
        + [jax.ShapeDtypeStruct((half, width), f32)] * members,
        input_output_aliases=aliases,
        compiler_params=params(),
        cost_estimate=cost(
            flops=2 * rows * tokens * width * members,
            bytes_accessed=(16 * rows * width + 3 * tokens * width) * members + 2 * tokens * rows,
            transcendentals=tokens * width * members,
        ),
        name="update_chunks",
    )(*args)
    return out[:2], out[2 : 2 + members], out[2 + members :]


def fold_kernel(kept, arrived, sent, left):
    total = kept[...] + get_code(arrived)
    half = total.shape[0] // 2
    left[...] = total[0:half, :]
    put_code(sent, *encode(total[half:, :]))


def fold_chunk(kept, arrived):
    rows, width = kept.shape
    tile = tile_of(0, width)
    half = rows // 2
    spec = lambda n: pl.BlockSpec((n, tile), lambda j: (0, j))
    return pl.pallas_call(
        fold_kernel,
        grid=(width // tile,),
        in_specs=[spec(rows), spec(rows + SCALE_ROWS)],
        out_specs=[spec(half + SCALE_ROWS), spec(half)],
        out_shape=[jax.ShapeDtypeStruct((half + SCALE_ROWS, width), bf16), jax.ShapeDtypeStruct((half, width), f32)],
        compiler_params=params(),
        cost_estimate=cost(
            flops=20 * rows * width, bytes_accessed=9 * rows * width, transcendentals=2 * rows * width
        ),
        name="fold_chunk",
    )(kept, arrived)


def hidden_kernel(kept, arrived, *refs):
    refs[-1][...] = (kept[...] + get_code(arrived)).astype(bf16)


def hidden_chunk(kept, arrived, before, start, columns):
    rows, width = kept.shape
    tile = tile_of(start, width)
    at = start // tile
    spec = lambda n: pl.BlockSpec((n, tile), lambda j: (0, j))
    args, in_specs, aliases = [kept, arrived], [spec(rows), spec(rows + SCALE_ROWS)], {}
    if before is not None:
        aliases = {2: 0}
        args.append(before)
        in_specs.append(pl.BlockSpec(memory_space=pl.ANY))
    return pl.pallas_call(
        hidden_kernel,
        grid=(width // tile,),
        in_specs=in_specs,
        out_specs=pl.BlockSpec((rows, tile), lambda j: (0, at + j)),
        out_shape=jax.ShapeDtypeStruct((rows, columns), bf16),
        input_output_aliases=aliases,
        compiler_params=params(),
        cost_estimate=cost(
            flops=10 * rows * width, bytes_accessed=8 * rows * width, transcendentals=rows * width
        ),
        name="hidden_chunk",
    )(*args)


def turn_features(blocks, dp, mp):
    inner = mp // dp
    me, outer = lax.axis_index("dp"), lax.axis_index("mp") // inner
    quarter = blocks.shape[1] // dp
    pick = lambda k: lax.dynamic_slice_in_dim(blocks, (outer ^ k) * quarter, quarter, axis=1)
    got = jnp.stack([pick(0)] + [swap(pick(k), "mp", mp, k * inner) for k in range(1, dp)])
    pick = lambda n: lax.dynamic_index_in_dim(got, outer ^ me ^ n, 0, keepdims=False)
    return [pick(0)] + [swap(pick(n), "dp", dp, n) for n in range(1, dp)]


def spread_features(block, dp, mp):
    return lax.all_gather(block, "mp", axis=0).reshape((dp, mp // dp) + block.shape)


def cut(columns, shares):
    unit = columns // sum(shares)
    widths = [LANES] * (columns // LANES) if unit % LANES else [unit * n for n in shares]
    return [(sum(widths[:c]), width) for c, width in enumerate(widths)]


def tile_of(start, width):
    return 256 if start % 256 == 0 and width % 256 == 0 else LANES


class Links:
    def __init__(self, dp):
        self.dp = dp
        self.past = {bit: [] for bit in bit_order(dp, 0)}

    def swap(self, value, bit):
        past = self.past[bit]
        if len(past) >= 2:
            value, _ = lax.optimization_barrier((value, past[-2]))
        past.append(swap(value, "dp", self.dp, bit))
        return past[-1]


def body(dp, mp, activations, out_grads, weight, row_state, column_state, next_batch):
    rows, columns = weight.shape
    links = Links(dp)

    parts = cut(columns, GRADIENT_SHARES)
    edge = parts[2][0]
    ahead, behind = out_grads[:, :edge], out_grads[:, edge:]
    bits = bit_order(dp, 0)
    near_ahead = {bit: swap(ahead, "dp", dp, bit) for bit in bits}
    share = turn_features(jnp.stack([activations, next_batch]), dp, mp)
    share[1], near_ahead, behind = lax.optimization_barrier((share[1], near_ahead, behind))
    near_behind = {bit: swap(behind, "dp", dp, bit) for bit in bits}
    share = jnp.stack(share)
    left = spread_features(share[:, 0].transpose(0, 2, 1), dp, mp)
    features = spread_features(share[:, 1], dp, mp)
    weight_total = jnp.sum(jnp.sum(weight * weight, axis=0))
    left, weight_total, near_behind = lax.optimization_barrier((left, weight_total, near_behind))

    far = [{} for _ in parts]
    for step in range(1, len(bit_order(dp, 0))):
        for c, (start, width) in enumerate(parts):
            bits = bit_order(dp, c)
            known = [0]
            for bit in bits[:step]:
                known = known + [n ^ bit for n in known]
            for n in known[1:]:
                near, at = (near_ahead, start) if start < edge else (near_behind, start - edge)
                block = far[c][n] if n in far[c] else near[n][:, at : at + width]
                far[c][n ^ bits[step]] = swap(block, "dp", dp, bits[step])
    before = None
    for (start, width), blocks in zip(parts, far):
        near, offset = (near_ahead, 0) if start < edge else (near_behind, edge)
        before = gradient_chunk(left, out_grads, near, blocks, before, start, offset, width)
    gradient, row_part, column_part = before

    row_sum = all_sum(jnp.sum(row_part, axis=1), "mp", mp)
    column_sum = all_sum(column_part[0], "dp", dp)
    row_moment = decay_rate * row_state + (1.0 - decay_rate) * (row_sum / (columns * mp))
    column_moment = decay_rate * column_state + (1.0 - decay_rate) * (column_sum / (rows * dp))

    raw_columns = jnp.sum(gradient * gradient * (1.0 / row_moment)[:, None], axis=0)
    raw_total = jnp.sum(raw_columns / column_moment)
    totals = jnp.where(jnp.arange(LANES) == 0, raw_total, weight_total)
    totals = all_sum(all_sum(totals, "mp", mp), "dp", dp)
    entries = rows * dp * columns * mp
    rms_update = jnp.sqrt(totals[0] / entries)
    rms_weight = jnp.sqrt(totals[1] / entries + weight_eps)
    row_scale = lax.rsqrt(row_moment)[:, None]
    column_scale = (lax.rsqrt(column_moment) / jnp.maximum(1.0, rms_update / clip_level))[None, :]
    step = (learn_rate * rms_weight).reshape(1, 1)

    parts = cut(columns, UPDATE_SHARES)
    links = Links(dp)
    written, hidden = None, None
    pending = []
    ways = len(bit_order(dp, 0))
    for c in range(0, len(parts), ways):
        orders = []
        for member in range(c, min(c + ways, len(parts))):
            order = [0]
            for bit in reversed(bit_order(dp, member)):
                order = order + [n ^ bit for n in order]
            orders.append(order)
        start, width = parts[c]
        written, sent, kept = update_chunks(
            gradient, weight, row_scale, column_scale, step, features, written, start, width, orders
        )
        for g in range(len(orders)):
            pending.append((kept[g], links.swap(sent[g], bit_order(dp, c + g)[0])))
    for step in range(1, len(bit_order(dp, 0))):
        for c, (kept, arrived) in enumerate(pending):
            sent, kept = fold_chunk(kept, arrived)
            pending[c] = kept, links.swap(sent, bit_order(dp, c)[step])
    for (start, width), (kept, arrived) in zip(parts, pending):
        hidden = hidden_chunk(kept, arrived, hidden, start, columns)
    new_weight, update = written
    return (new_weight, update, row_moment, column_moment, hidden)


def solution(mesh):
    return jax.shard_map(
        functools.partial(body, mesh.shape["dp"], mesh.shape["mp"]),
        mesh=mesh,
        in_specs=(P("dp", "mp"), P("dp", "mp"), P("dp", "mp"), P("dp"), P("mp"), P("dp", "mp")),
        out_specs=(P("dp", "mp"), P("dp", "mp"), P("dp"), P("mp"), P("dp", "mp")),
        check_vma=False,
    )
```

profile of v0, /device:TPU:0, one launch (start us, length us, event | category | flops | bytes accessed | tf_op | source)
XLA Modules:
  0.0 377.2 jit_solution(14199319488483412962)
XLA Ops:
  7.2 2.7 slice.36
  9.9 3.0 collective-permute-start.5
  12.8 1.5 collective-permute-start.4
  14.3 2.0 copy.40
  16.4 2.0 copy.41
  18.4 2.3 fusion.2
  20.7 1.6 collective-permute-start
  22.3 2.6 collective-permute-start.1
  25.1 8.0 %collective-permute-done = bf16[2,128,512]{1,2,0:T(8,128)(2,1)} collective-permute-done((bf16[2,128,512]{1,2,0:T(8,128)(2,1)}, bf16[2,128,512]{1,2,0:T(8,128)(2,1)}, u32[]{:S(2)}, u32[]{:S(2)}) %collective-permute-start) | collective-permute-done | bytes 262176 | tf_op jit(solution)/shard_map/ppermute | solution.py:26
  33.0 10.9 %collective-permute-done.1 = bf16[2,128,512]{1,2,0:T(8,128)(2,1)} collective-permute-done((bf16[2,128,512]{1,2,0:T(8,128)(2,1)}, bf16[2,128,512]{1,2,0:T(8,128)(2,1)}, u32[]{:S(2)}, u32[]{:S(2)}) %collective-permute-start.1) | collective-permute-done | bytes 262176 | tf_op jit(solution)/shard_map/ppermute | solution.py:26
  47.3 1.5 collective-permute-start.6
  48.8 1.7 slice.37
  50.5 5.4 %collective-permute-done.3 = bf16[2,128,512]{1,2,0:T(8,128)(2,1)S(1)} collective-permute-done((bf16[2,128,512]{1,2,0:T(8,128)(2,1)S(1)}, bf16[2,128,512]{1,2,0:T(8,128)(2,1)S(1)}, u32[]{:S(2)}, u32[]{:S(2)}) %collective-permute-start.3) | collective-permute-done | bytes 262176 | tf_op jit(solution)/shard_map/ppermute | solution.py:26
  56.0 3.9 %collective-permute-done.7 = bf16[2,128,512]{1,2,0:T(8,128)(2,1)S(1)} collective-permute-done((bf16[2,128,512]{1,2,0:T(8,128)(2,1)S(1)}, bf16[2,128,512]{1,2,0:T(8,128)(2,1)S(1)}, u32[]{:S(2)}, u32[]{:S(2)}) %collective-permute-start.7) | collective-permute-done | bytes 262176 | tf_op jit(solution)/shard_map/ppermute | solution.py:26
  61.2 2.1 copy.44
  63.3 1.8 collective-permute-start.9
  65.1 1.5 collective-permute-start.8
  66.6 2.1 slice.44
  68.7 2.2 slice.43
  71.6 10.7 %multiply_reduce_fusion.1 = f32[]{:T(128)} fusion(f32[1024,4096]{1,0:T(8,128)} %weight.7), kind=kLoop, calls=%fused_computation.1 | loop fusion | flops 8388607 | bytes 16777220 | tf_op jit(solution)/shard_map/reduce_sum | solution.py:334
  82.3 41.0 %collective-permute-done.9.refs_3_ = bf16[512,2560]{1,0:T(8,128)(2,1)S(1)} collective-permute-done((bf16[512,2560]{1,0:T(8,128)(2,1)}, bf16[512,2560]{1,0:T(8,128)(2,1)S(1)}, u32[]{:S(2)}, u32[]{:S(2)}) %collective-permute-start.9) | collective-permute-done | bytes 2621472 | tf_op jit(solution)/shard_map/ppermute | solution.py:26
  123.3 1.8 collective-permute-done.8.refs_2_
  126.9 1.8 collective-permute-start.12
  129.8 1.6 collective-permute-start.11
  131.5 8.7 %collective-permute-done.15.refs_4_ = bf16[512,768]{1,0:T(8,128)(2,1)S(1)} collective-permute-done((bf16[512,768]{1,0:T(8,128)(2,1)}, bf16[512,768]{1,0:T(8,128)(2,1)S(1)}, u32[]{:S(2)}, u32[]{:S(2)}) %collective-permute-start.15) | collective-permute-done | bytes 786464 | tf_op jit(solution)/shard_map/ppermute | solution.py:26
  140.2 1.7 collective-permute-start.10
  141.9 2.3 copy-done.2
  145.6 1.4 copy-done.7
  147.0 5.5 %gradient_chunk.6 = (f32[1024,4096]{1,0:T(8,128)}, f32[1024,128]{1,0:T(8,128)S(1)}, f32[1,4096]{1,0:T(1,128)S(1)}) custom-call(bf16[4,2,4,512,128]{4,3,2,1,0:T(8,128)(2,1)S(1)} %bitcast.31, bf16[512,4096]{1,0:T(8,128)(2,1)S(1)} %copy-done.1, bf16[512,1536]{1,0:T(8,128)(2,1)S(1)} %copy-done.7, bf16[512,1536]{1,0:T(8,128)(2,1)S(1)} %copy-done.5, ...), custom_call_target="tpu_custom_call" | custom-call | flops 32212254 | bytes 104857 | tf_op jit(solution)/shard_map/gradient_chunk/pallas_call | solution.py:131
  152.5 6.3 %gradient_chunk.7 = (f32[1024,4096]{1,0:T(8,128)}, f32[1024,128]{1,0:T(8,128)S(1)}, f32[1,4096]{1,0:T(1,128)S(1)}) custom-call(bf16[4,2,4,512,128]{4,3,2,1,0:T(8,128)(2,1)S(1)} %bitcast.32, bf16[512,4096]{1,0:T(8,128)(2,1)S(1)} %copy-done.1, bf16[512,1536]{1,0:T(8,128)(2,1)S(1)} %copy-done.7, ...), custom_call_target="tpu_custom_call", output_to_operand_aliasing={{0}: (6, {}), {2}: (7, {})} | custom-call | flops 32212254 | bytes 104857 | tf_op jit(solution)/shard_map/gradient_chunk/pallas_call | solution.py:131
  158.8 6.2 %gradient_chunk.8 = (f32[1024,4096]{1,0:T(8,128)}, f32[1024,128]{1,0:T(8,128)S(1)}, f32[1,4096]{1,0:T(1,128)S(1)}) custom-call(bf16[4,2,4,512,128]{4,3,2,1,0:T(8,128)(2,1)S(1)} %bitcast.33, bf16[512,4096]{1,0:T(8,128)(2,1)S(1)} %copy-done.1, bf16[512,2560]{1,0:T(8,128)(2,1)} %collective-permute-done.8.refs_2_, ...), custom_call_target="tpu_custom_call", output_to_operand_aliasing={{0}: (6, {}), {2}: (7, {})} | custom-call | flops 32212254 | bytes 104857 | tf_op jit(solution)/shard_map/gradient_chunk/pallas_call | solution.py:131
  165.1 6.3 %gradient_chunk.9 = (f32[1024,4096]{1,0:T(8,128)}, f32[1024,128]{1,0:T(8,128)S(1)}, f32[1,4096]{1,0:T(1,128)S(1)}) custom-call(bf16[4,2,4,512,128]{4,3,2,1,0:T(8,128)(2,1)S(1)} %bitcast.34, bf16[512,4096]{1,0:T(8,128)(2,1)S(1)} %copy-done.1, bf16[512,2560]{1,0:T(8,128)(2,1)} %collective-permute-done.8.refs_2_, ...), custom_call_target="tpu_custom_call", output_to_operand_aliasing={{0}: (6, {}), {2}: (7, {})} | custom-call | flops 32212254 | bytes 104857 | tf_op jit(solution)/shard_map/gradient_chunk/pallas_call | solution.py:131
  171.3 4.8 %gradient_chunk.10 = (f32[1024,4096]{1,0:T(8,128)}, f32[1024,128]{1,0:T(8,128)S(1)}, f32[1,4096]{1,0:T(1,128)S(1)}) custom-call(bf16[4,2,4,512,128]{4,3,2,1,0:T(8,128)(2,1)S(1)} %bitcast.35, bf16[512,4096]{1,0:T(8,128)(2,1)S(1)} %copy-done.1, bf16[512,2560]{1,0:T(8,128)(2,1)} %collective-permute-done.8.refs_2_, ...), custom_call_target="tpu_custom_call", output_to_operand_aliasing={{0}: (6, {}), {2}: (7, {})} | custom-call | flops 21474836 | bytes 83886 | tf_op jit(solution)/shard_map/gradient_chunk/pallas_call | solution.py:131
  176.1 4.8 %gradient_chunk.11 = (f32[1024,4096]{1,0:T(8,128)}, f32[1024,128]{1,0:T(8,128)S(1)}, f32[1,4096]{1,0:T(1,128)S(1)}) custom-call(bf16[4,2,4,512,128]{4,3,2,1,0:T(8,128)(2,1)S(1)} %bitcast.36, bf16[512,4096]{1,0:T(8,128)(2,1)S(1)} %copy-done.1, bf16[512,2560]{1,0:T(8,128)(2,1)} %collective-permute-done.8.refs_2_, ...), custom_call_target="tpu_custom_call", output_to_operand_aliasing={{0}: (6, {}), {2}: (7, {})} | custom-call | flops 21474836 | bytes 83886 | tf_op jit(solution)/shard_map/gradient_chunk/pallas_call | solution.py:131
  181.2 2.5 collective-permute-start.17
  185.3 3.1 collective-permute-start.19
  188.4 1.7 collective-permute-start.22
  192.0 7.7 %multiply_reduce_fusion = f32[4096]{0:T(1024)S(1)} fusion(f32[1024,4096]{1,0:T(8,128)} %get-tuple-element.105.gradient, f32[1024]{0:T(1024)S(1)} %broadcast_divide_fusion), kind=kLoop, calls=%fused_computation | loop fusion | flops 12578816 | bytes 16797696 | tf_op jit(solution)/shard_map/reduce_sum | solution.py:359
  202.3 1.5 collective-permute-start.23
  207.8 3.2 collective-permute-done.26
  211.0 1.6 collective-permute-start.29
  218.7 2.2 copy-done.3
  220.9 7.0 %update_chunks.4 = (f32[1024,4096]{1,0:T(8,128)}, f32[1024,4096]{1,0:T(8,128)}, bf16[1040,256]{1,0:T(8,128)(2,1)S(1)}, bf16[1040,256]{1,0:T(8,128)(2,1)S(1)}, f3...) custom-call(f32[1,1]{1,0:T(1,128)} %bitcast.18.step, f32[1024,4096]{1,0:T(8,128)} %get-tuple-element.105.gradient, ...), custom_call_target="tpu_custom_call" | custom-call | flops 21474836 | bytes 157286 | tf_op jit(solution)/shard_map/update_chunks/pallas_call | solution.py:205
  227.9 1.6 collective-permute-start.38
  230.8 11.7 %update_chunks.5 = (f32[1024,4096]{1,0:T(8,128)}, f32[1024,4096]{1,0:T(8,128)}, bf16[1040,512]{1,0:T(8,128)(2,1)S(1)}, bf16[1040,512]{1,0:T(8,128)(2,1)}, f32[10...) custom-call(f32[1,1]{1,0:T(1,128)} %bitcast.18.step, ...), custom_call_target="tpu_custom_call", output_to_operand_aliasing={{0}: (6, {}), {1}: (7, {})} | custom-call | flops 42949672 | bytes 272629 | tf_op jit(solution)/shard_map/update_chunks/pallas_call | solution.py:205
  243.8 16.7 %update_chunks.6 = (f32[1024,4096]{1,0:T(8,128)}, f32[1024,4096]{1,0:T(8,128)}, bf16[1040,768]{1,0:T(8,128)(2,1)}, bf16[1040,768]{1,0:T(8,128)(2,1)}, f32[1024,768]{1,0:T(8,128)S(1)}, /*index=5*/f32[1024,768]{1,0:T(8,128)S(1)}) custom-call(f32[1,1]{1,0:T(1,128)} %bitcast.18.step, ...), custom_call_target="tpu_custom_call", output_to_operand_aliasing={{0}: (6, {}), {1}: (7, {})} | custom-call | flops 64424508 | bytes 387973 | tf_op jit(solution)/shard_map/update_chunks/pallas_call | solution.py:205
  262.7 1.4 collective-permute-start.39
  264.1 11.7 %update_chunks.7 = (f32[1024,4096]{1,0:T(8,128)}, f32[1024,4096]{1,0:T(8,128)}, bf16[1040,512]{1,0:T(8,128)(2,1)S(1)}, bf16[1040,512]{1,0:T(8,128)(2,1)}, f32[10...) custom-call(f32[1,1]{1,0:T(1,128)} %bitcast.18.step, ...), custom_call_target="tpu_custom_call", output_to_operand_aliasing={{0}: (6, {}), {1}: (7, {})} | custom-call | flops 42949672 | bytes 272629 | tf_op jit(solution)/shard_map/update_chunks/pallas_call | solution.py:205
  282.0 1.9 fold_chunk.9
  283.9 1.9 fold_chunk.11
  285.9 17.9 %collective-permute-done.41.arrived = bf16[1040,768]{1,0:T(8,128)(2,1)S(1)} collective-permute-done((bf16[1040,768]{1,0:T(8,128)(2,1)}, bf16[1040,768]{1,0:T(8,128)(2,1)S(1)}, u32[]{:S(2)}, u32[]{:S(2)}) %collective-permute-start.41) | collective-permute-done | bytes 1597472 | tf_op jit(solution)/shard_map/ppermute | solution.py:26
  304.4 1.5 collective-permute-start.44
  305.9 19.2 %collective-permute-done.31.arrived = bf16[1040,512]{1,0:T(8,128)(2,1)S(1)} collective-permute-done((bf16[1040,512]{1,0:T(8,128)(2,1)}, bf16[1040,512]{1,0:T(8,128)(2,1)S(1)}, u32[]{:S(2)}, u32[]{:S(2)}) %collective-permute-start.31) | collective-permute-done | bytes 1064992 | tf_op jit(solution)/shard_map/ppermute | solution.py:26
  325.0 1.5 collective-permute-done.33.arrived
  327.2 2.9 fold_chunk.14
  330.1 4.2 %fold_chunk.12 = (bf16[528,768]{1,0:T(8,128)(2,1)S(1)}, f32[512,768]{1,0:T(8,128)S(1)}) custom-call(f32[1024,768]{1,0:T(8,128)S(1)} %get-tuple-element.137.kept, bf16[1040,768]{1,0:T(8,128)(2,1)} %collective-permute-done.39.arrived), custom_call_target="tpu_custom_call" | custom-call | flops 157286 | bytes 70778 | tf_op jit(solution)/shard_map/fold_chunk/pallas_call | solution.py:239
  334.3 1.6 collective-permute-start.45
  337.2 1.9 fold_chunk.10
  339.2 1.9 fold_chunk.8
  342.4 1.5 collective-permute-done.34.arrived
  348.9 10.9 %collective-permute-done.45.arrived = bf16[528,768]{1,0:T(8,128)(2,1)S(1)} collective-permute-done((bf16[528,768]{1,0:T(8,128)(2,1)S(1)}, bf16[528,768]{1,0:T(8,128)(2,1)S(1)}, u32[]{:S(2)}, u32[]{:S(2)}) %collective-permute-start.45) | collective-permute-done | bytes 811040 | tf_op jit(solution)/shard_map/ppermute | solution.py:26
  359.8 1.9 hidden_chunk.12.refs_0_
  361.7 1.9 hidden_chunk.13.refs_0_
  363.7 4.2 %collective-permute-done.37.arrived = bf16[528,512]{1,0:T(8,128)(2,1)S(1)} collective-permute-done((bf16[528,512]{1,0:T(8,128)(2,1)S(1)}, bf16[528,512]{1,0:T(8,128)(2,1)S(1)}, u32[]{:S(2)}, u32[]{:S(2)}) %collective-permute-start.37) | collective-permute-done | bytes 540704 | tf_op jit(solution)/shard_map/ppermute | solution.py:26
  (124 shorter events, 47.1 us)
Async XLA Ops:
  7.2 118.0 %all-gather.5.cloned.1.call-start = ((), (), s32[]{:S(2)}) async-start(), calls=%async_computation | async-start | bytes 4718592 | tf_op jit(solution)/shard_map/all_gather | solution.py:293
  9.9 46.1 %collective-permute-start.5 = (bf16[512,1536]{1,0:T(8,128)(2,1)}, bf16[512,1536]{1,0:T(8,128)(2,1)S(1)}, u32[]{:S(2)}, u32[]{:S(2)}) collective-permute-start(bf16[512,1536]{1,0:T(8,128)(2,1)} %slice.36), channel_id=1, source_target_pairs={{0,16},{8,24},{16,0},{24,8},{1,17},{9,25},{17,1},{25,9},{2,18},{10... | collective-permute-start | bytes 4718600 | tf_op jit(solution)/shard_map/ppermute | solution.py:26
  12.8 43.2 %collective-permute-start.4 = (bf16[512,1536]{1,0:T(8,128)(2,1)}, bf16[512,1536]{1,0:T(8,128)(2,1)S(1)}, u32[]{:S(2)}, u32[]{:S(2)}) collective-permute-start(bf16[512,1536]{1,0:T(8,128)(2,1)} %slice.36), channel_id=1, source_target_pairs={{0,8},{8,0},{16,24},{24,16},{1,9},{9,1},{17,25},{25,17},{2,10},{10... | collective-permute-start | bytes 4718600 | tf_op jit(solution)/shard_map/ppermute | solution.py:26
  20.7 12.4 %collective-permute-start = (bf16[2,128,512]{1,2,0:T(8,128)(2,1)}, bf16[2,128,512]{1,2,0:T(8,128)(2,1)}, u32[]{:S(2)}, u32[]{:S(2)}) collective-permute-start(bf16[2,128,512]{1,2,0:T(8,128)(2,1)} %get-tuple-element.172), channel_id=1, source_target_pairs={{0,2},{1,3},{2,0},{3,1},{4,6},{5,7},{6,4},{7,5},{8,10},{9,11},{10,... | collective-permute-start | bytes 786440 | tf_op jit(solution)/shard_map/ppermute | solution.py:26
  22.3 21.7 %collective-permute-start.1 = (bf16[2,128,512]{1,2,0:T(8,128)(2,1)}, bf16[2,128,512]{1,2,0:T(8,128)(2,1)}, u32[]{:S(2)}, u32[]{:S(2)}) collective-permute-start(bf16[2,128,512]{1,2,0:T(8,128)(2,1)} %get-tuple-element.173), channel_id=1, source_target_pairs={{0,4},{1,5},{2,6},{3,7},{4,0},{5,1},{6,2},{7,3},{8,12},{9,13},{10,... | collective-permute-start | bytes 786440 | tf_op jit(solution)/shard_map/ppermute | solution.py:26
  24.8 19.1 %collective-permute-start.2 = (bf16[2,128,512]{1,2,0:T(8,128)(2,1)}, bf16[2,128,512]{1,2,0:T(8,128)(2,1)}, u32[]{:S(2)}, u32[]{:S(2)}) collective-permute-start(bf16[2,128,512]{1,2,0:T(8,128)(2,1)} %get-tuple-element.174), channel_id=1, source_target_pairs={{0,6},{1,7},{2,4},{3,5},{4,2},{5,3},{6,0},{7,1},{8,14},{9,15},{10,... | collective-permute-start | bytes 786440 | tf_op jit(solution)/shard_map/ppermute | solution.py:26
  25.1 23.8 %copy-start = (bf16[512,4096]{1,0:T(8,128)(2,1)S(1)}, bf16[512,4096]{1,0:T(8,128)(2,1)}, u32[]{:S(2)}) copy-start(bf16[512,4096]{1,0:T(8,128)(2,1)} %refs_1_.11) | copy-start | bytes 12582916
  45.3 10.7 %collective-permute-start.3 = (bf16[2,128,512]{1,2,0:T(8,128)(2,1)S(1)}, bf16[2,128,512]{1,2,0:T(8,128)(2,1)S(1)}, u32[]{:S(2)}, u32[]{:S(2)}) collective-permute-start(bf16[2,128,512]{1,2,0:T(8,128)(2,1)S(1)} %get-tuple-element.170), channel_id=1, source_target_pairs={{0,8},{8,0},{16,24},{24,16},{1,9},{9,1},{17,25},{25,17},{2,10},{10... | collective-permute-start | bytes 786440 | tf_op jit(solution)/shard_map/ppermute | solution.py:26
  45.9 14.0 %collective-permute-start.7 = (bf16[2,128,512]{1,2,0:T(8,128)(2,1)S(1)}, bf16[2,128,512]{1,2,0:T(8,128)(2,1)S(1)}, u32[]{:S(2)}, u32[]{:S(2)}) collective-permute-start(bf16[2,128,512]{1,2,0:T(8,128)(2,1)S(1)} %get-tuple-element.168), channel_id=1, source_target_pairs={{0,24},{8,16},{16,8},{24,0},{1,25},{9,17},{17,9},{25,1},{2,26},{10... | collective-permute-start | bytes 786440 | tf_op jit(solution)/shard_map/ppermute | solution.py:26
  47.3 12.5 %collective-permute-start.6 = (bf16[2,128,512]{1,2,0:T(8,128)(2,1)S(1)}, bf16[2,128,512]{1,2,0:T(8,128)(2,1)S(1)}, u32[]{:S(2)}, u32[]{:S(2)}) collective-permute-start(bf16[2,128,512]{1,2,0:T(8,128)(2,1)S(1)} %get-tuple-element.169), channel_id=1, source_target_pairs={{0,16},{8,24},{16,0},{24,8},{1,17},{9,25},{17,1},{25,9},{2,18},{10... | collective-permute-start | bytes 786440 | tf_op jit(solution)/shard_map/ppermute | solution.py:26
  56.0 7.3 %copy-start.4 = (bf16[512,1536]{1,0:T(8,128)(2,1)}, bf16[512,1536]{1,0:T(8,128)(2,1)S(1)}, u32[]{:S(2)}) copy-start(bf16[512,1536]{1,0:T(8,128)(2,1)S(1)} %collective-permute-done.5.refs_3_) | copy-start | bytes 4718596
  56.0 7.3 %copy-start.6 = (bf16[512,1536]{1,0:T(8,128)(2,1)}, bf16[512,1536]{1,0:T(8,128)(2,1)S(1)}, u32[]{:S(2)}) copy-start(bf16[512,1536]{1,0:T(8,128)(2,1)S(1)} %collective-permute-done.4.refs_2_) | copy-start | bytes 4718596
  61.1 157.6 %all-gather.7.cloned.1.call-start = ((), (), s32[]{:S(2)}) async-start(), calls=%async_computation.1 | async-start | bytes 4718592 | tf_op jit(solution)/shard_map/all_gather | solution.py:293
  63.3 60.1 %collective-permute-start.9 = (bf16[512,2560]{1,0:T(8,128)(2,1)}, bf16[512,2560]{1,0:T(8,128)(2,1)S(1)}, u32[]{:S(2)}, u32[]{:S(2)}) collective-permute-start(bf16[512,2560]{1,0:T(8,128)(2,1)} %slice.37), channel_id=1, source_target_pairs={{0,16},{8,24},{16,0},{24,8},{1,17},{9,25},{17,1},{25,9},{2,18},{10... | collective-permute-start | bytes 7864328 | tf_op jit(solution)/shard_map/ppermute | solution.py:26
  65.1 60.1 %collective-permute-start.8 = (bf16[512,2560]{1,0:T(8,128)(2,1)}, bf16[512,2560]{1,0:T(8,128)(2,1)}, u32[]{:S(2)}, u32[]{:S(2)}) collective-permute-start(bf16[512,2560]{1,0:T(8,128)(2,1)} %slice.37), channel_id=1, source_target_pairs={{0,8},{8,0},{16,24},{24,16},{1,9},{9,1},{17,25},{25,17},{2,10},{10... | collective-permute-start | bytes 7864328 | tf_op jit(solution)/shard_map/ppermute | solution.py:26
  70.8 81.7 %collective-permute-start.14 = (bf16[512,768]{1,0:T(8,128)(2,1)}, bf16[512,768]{1,0:T(8,128)(2,1)}, u32[]{:S(2)}, u32[]{:S(2)}) collective-permute-start(bf16[512,768]{1,0:T(8,128)(2,1)} %slice.43), channel_id=1, source_target_pairs={{0,8},{8,0},{16,24},{24,16},{1,9},{9,1},{17,25},{25,17},{2,10},{10... | collective-permute-start | bytes 2359304 | tf_op jit(solution)/shard_map/ppermute | solution.py:26
  71.3 68.9 %collective-permute-start.15 = (bf16[512,768]{1,0:T(8,128)(2,1)}, bf16[512,768]{1,0:T(8,128)(2,1)S(1)}, u32[]{:S(2)}, u32[]{:S(2)}) collective-permute-start(bf16[512,768]{1,0:T(8,128)(2,1)} %slice.44), channel_id=1, source_target_pairs={{0,16},{8,24},{16,0},{24,8},{1,17},{9,25},{17,1},{25,9},{2,18},{10... | collective-permute-start | bytes 2359304 | tf_op jit(solution)/shard_map/ppermute | solution.py:26
  125.2 16.7 %copy-start.1 = (bf16[512,4096]{1,0:T(8,128)(2,1)S(1)}, bf16[512,4096]{1,0:T(8,128)(2,1)}, u32[]{:S(2)}) copy-start(bf16[512,4096]{1,0:T(8,128)(2,1)} %refs_1_.11) | copy-start | bytes 12582916
  126.6 32.3 %collective-permute-start.13 = (bf16[512,768]{1,0:T(8,128)(2,1)S(1)}, bf16[512,768]{1,0:T(8,128)(2,1)S(1)}, u32[]{:S(2)}, u32[]{:S(2)}) collective-permute-start(bf16[512,768]{1,0:T(8,128)(2,1)S(1)} %slice.42), channel_id=1, source_target_pairs={{0,16},{8,24},{16,0},{24,8},{1,17},{9,25},{17,1},{25,9},{2,18},{10... | collective-permute-start | bytes 2359304 | tf_op jit(solution)/shard_map/ppermute | solution.py:26
  126.9 38.1 %collective-permute-start.12 = (bf16[512,768]{1,0:T(8,128)(2,1)S(1)}, bf16[512,768]{1,0:T(8,128)(2,1)S(1)}, u32[]{:S(2)}, u32[]{:S(2)}) collective-permute-start(bf16[512,768]{1,0:T(8,128)(2,1)S(1)} %slice.41), channel_id=1, source_target_pairs={{0,8},{8,0},{16,24},{24,16},{1,9},{9,1},{17,25},{25,17},{2,10},{10... | collective-permute-start | bytes 2359304 | tf_op jit(solution)/shard_map/ppermute | solution.py:26
  129.8 41.5 %collective-permute-start.11 = (bf16[512,512]{1,0:T(8,128)(2,1)S(1)}, bf16[512,512]{1,0:T(8,128)(2,1)S(1)}, u32[]{:S(2)}, u32[]{:S(2)}) collective-permute-start(bf16[512,512]{1,0:T(8,128)(2,1)S(1)} %slice.40), channel_id=1, source_target_pairs={{0,16},{8,24},{16,0},{24,8},{1,17},{9,25},{17,1},{25,9},{2,18},{10... | collective-permute-start | bytes 1572872 | tf_op jit(solution)/shard_map/ppermute | solution.py:26
  140.2 35.9 %collective-permute-start.10 = (bf16[512,512]{1,0:T(8,128)(2,1)S(1)}, bf16[512,512]{1,0:T(8,128)(2,1)S(1)}, u32[]{:S(2)}, u32[]{:S(2)}) collective-permute-start(bf16[512,512]{1,0:T(8,128)(2,1)S(1)} %slice.39), channel_id=1, source_target_pairs={{0,8},{8,0},{16,24},{24,16},{1,9},{9,1},{17,25},{25,17},{2,10},{10... | collective-permute-start | bytes 1572872 | tf_op jit(solution)/shard_map/ppermute | solution.py:26
  141.9 2.3 copy-start.2
  144.2 1.4 copy-start.5
  145.6 1.4 copy-start.7
  176.1 15.8 %copy-start.16 = (f32[1024]{0:T(1024)S(1)}, f32[1024]{0:T(1024)}, u32[]{:S(2)}) copy-start(f32[1024]{0:T(1024)} %param.9) | copy-start | bytes 12292
  181.1 3.1 collective-permute-start.18
  181.2 4.1 %collective-permute-start.17 = (f32[1024]{0:T(1024)S(1)}, f32[1024]{0:T(1024)S(1)}, u32[]{:S(2)}, u32[]{:S(2)}) collective-permute-start(f32[1024]{0:T(1024)S(1)} %reduce_sum.41), channel_id=1, source_target_pairs={{0,2},{1,3},{2,0},{3,1},{4,6},{5,7},{6,4},{7,5},{8,10},{9,11},{10,... | collective-permute-start | bytes 12296 | tf_op jit(solution)/shard_map/ppermute | solution.py:26
  183.7 1.6 collective-permute-start.16
  185.3 6.6 %collective-permute-start.19 = (f32[1024]{0:T(1024)S(1)}, f32[1024]{0:T(1024)S(1)}, u32[]{:S(2)}, u32[]{:S(2)}) collective-permute-start(f32[1024]{0:T(1024)S(1)} %add_add_fusion), channel_id=1, source_target_pairs={{0,4},{1,5},{2,6},{3,7},{4,0},{5,1},{6,2},{7,3},{8,12},{9,13},{10,... | collective-permute-start | bytes 12296 | tf_op jit(solution)/shard_map/ppermute | solution.py:26
  188.4 11.3 %collective-permute-start.22 = (f32[4096]{0:T(1024)S(1)}, f32[4096]{0:T(1024)S(1)}, u32[]{:S(2)}, u32[]{:S(2)}) collective-permute-start(f32[4096]{0:T(1024)S(1)} %bitcast.41), channel_id=1, source_target_pairs={{0,24},{8,16},{16,8},{24,0},{1,25},{9,17},{17,9},{25,1},{2,26},{10... | collective-permute-start | bytes 49160 | tf_op jit(solution)/shard_map/ppermute | solution.py:26
  190.2 9.5 %collective-permute-start.21 = (f32[4096]{0:T(1024)S(1)}, f32[4096]{0:T(1024)S(1)}, u32[]{:S(2)}, u32[]{:S(2)}) collective-permute-start(f32[4096]{0:T(1024)S(1)} %bitcast.42), channel_id=1, source_target_pairs={{0,16},{8,24},{16,0},{24,8},{1,17},{9,25},{17,1},{25,9},{2,18},{10... | collective-permute-start | bytes 49160 | tf_op jit(solution)/shard_map/ppermute | solution.py:26
  190.7 9.0 %collective-permute-start.20 = (f32[4096]{0:T(1024)S(1)}, f32[4096]{0:T(1024)S(1)}, u32[]{:S(2)}, u32[]{:S(2)}) collective-permute-start(f32[4096]{0:T(1024)S(1)} %bitcast.43), channel_id=1, source_target_pairs={{0,8},{8,0},{16,24},{24,16},{1,9},{9,1},{17,25},{25,17},{2,10},{10... | collective-permute-start | bytes 49160 | tf_op jit(solution)/shard_map/ppermute | solution.py:26
  191.9 7.7 %copy-start.15 = (f32[1024]{0:T(1024)}, f32[1024]{0:T(1024)S(1)}, u32[]{:S(2)}) copy-start(f32[1024]{0:T(1024)S(1)} %get-tuple-element.162) | copy-start | bytes 12292
  192.0 7.8 %copy-start.14 = (f32[4096]{0:T(1024)S(1)}, f32[4096]{0:T(1024)}, u32[]{:S(2)}) copy-start(f32[4096]{0:T(1024)} %param.10) | copy-start | bytes 49156
  200.3 27.6 %copy-start.13 = (f32[4096]{0:T(1024)}, f32[4096]{0:T(1024)S(1)}, u32[]{:S(2)}) copy-start(f32[4096]{0:T(1024)S(1)} %get-tuple-element.164) | copy-start | bytes 49156
  201.6 3.6 collective-permute-start.24
  202.3 3.0 collective-permute-start.25
  202.3 3.0 collective-permute-start.23
  206.5 4.5 %collective-permute-start.26 = (f32[128]{0:T(128)S(1)}, f32[128]{0:T(128)S(1)}, u32[]{:S(2)}, u32[]{:S(2)}) collective-permute-start(f32[128]{0:T(128)S(1)} %add_add_fusion.2), channel_id=1, source_target_pairs={{0,4},{1,5},{2,6},{3,7},{4,0},{5,1},{6,2},{7,3},{8,12},{9,13},{10,... | collective-permute-start | bytes 1544 | tf_op jit(solution)/shard_map/ppermute | solution.py:26
  211.0 4.4 %collective-permute-start.29 = (f32[128]{0:T(128)S(1)}, f32[128]{0:T(128)S(1)}, u32[]{:S(2)}, u32[]{:S(2)}) collective-permute-start(f32[128]{0:T(128)S(1)} %add.98), channel_id=1, source_target_pairs={{0,24},{8,16},{16,8},{24,0},{1,25},{9,17},{17,9},{25,1},{2,26},{10... | collective-permute-start | bytes 1544 | tf_op jit(solution)/shard_map/ppermute | solution.py:26
  212.6 3.5 collective-permute-start.28
  213.1 3.5 collective-permute-start.27
  218.7 2.2 copy-start.3
  227.9 14.6 %copy-start.8 = (f32[1024,256]{1,0:T(8,128)}, f32[1024,256]{1,0:T(8,128)S(1)}, u32[]{:S(2)}) copy-start(f32[1024,256]{1,0:T(8,128)S(1)} %get-tuple-element.143.kept) | copy-start | bytes 3145732
  227.9 34.0 %collective-permute-start.38 = (bf16[1040,256]{1,0:T(8,128)(2,1)S(1)}, bf16[1040,256]{1,0:T(8,128)(2,1)S(1)}, u32[]{:S(2)}, u32[]{:S(2)}) collective-permute-start(bf16[1040,256]{1,0:T(8,128)(2,1)S(1)} %get-tuple-element.139), channel_id=1, source_target_pairs={{0,16},{8,24},{16,0},{24,8},{1,17},{9,25},{17,1},{25,9},{2,18},{10... | collective-permute-start | bytes 1597448 | tf_op jit(solution)/shard_map/ppermute | solution.py:26
  229.5 31.0 %collective-permute-start.40 = (bf16[1040,256]{1,0:T(8,128)(2,1)S(1)}, bf16[1040,256]{1,0:T(8,128)(2,1)S(1)}, u32[]{:S(2)}, u32[]{:S(2)}) collective-permute-start(bf16[1040,256]{1,0:T(8,128)(2,1)S(1)} %get-tuple-element.146), channel_id=1, source_target_pairs={{0,8},{8,0},{16,24},{24,16},{1,9},{9,1},{17,25},{25,17},{2,10},{10... | collective-permute-start | bytes 1597448 | tf_op jit(solution)/shard_map/ppermute | solution.py:26
  242.5 34.4 %collective-permute-start.30 = (bf16[1040,512]{1,0:T(8,128)(2,1)}, bf16[1040,512]{1,0:T(8,128)(2,1)S(1)}, u32[]{:S(2)}, u32[]{:S(2)}) collective-permute-start(bf16[1040,512]{1,0:T(8,128)(2,1)} %get-tuple-element.119), channel_id=1, source_target_pairs={{0,16},{8,24},{16,0},{24,8},{1,17},{9,25},{17,1},{25,9},{2,18},{10... | collective-permute-start | bytes 3194888 | tf_op jit(solution)/shard_map/ppermute | solution.py:26
  243.1 34.4 %collective-permute-start.32 = (bf16[1040,512]{1,0:T(8,128)(2,1)S(1)}, bf16[1040,512]{1,0:T(8,128)(2,1)S(1)}, u32[]{:S(2)}, u32[]{:S(2)}) collective-permute-start(bf16[1040,512]{1,0:T(8,128)(2,1)S(1)} %get-tuple-element.126), channel_id=1, source_target_pairs={{0,8},{8,0},{16,24},{24,16},{1,9},{9,1},{17,25},{25,17},{2,10},{10... | collective-permute-start | bytes 3194888 | tf_op jit(solution)/shard_map/ppermute | solution.py:26
  260.5 43.3 %collective-permute-start.41 = (bf16[1040,768]{1,0:T(8,128)(2,1)}, bf16[1040,768]{1,0:T(8,128)(2,1)S(1)}, u32[]{:S(2)}, u32[]{:S(2)}) collective-permute-start(bf16[1040,768]{1,0:T(8,128)(2,1)} %get-tuple-element.147), channel_id=1, source_target_pairs={{0,8},{8,0},{16,24},{24,16},{1,9},{9,1},{17,25},{25,17},{2,10},{10... | collective-permute-start | bytes 4792328 | tf_op jit(solution)/shard_map/ppermute | solution.py:26
  262.7 41.7 %collective-permute-start.39 = (bf16[1040,768]{1,0:T(8,128)(2,1)}, bf16[1040,768]{1,0:T(8,128)(2,1)}, u32[]{:S(2)}, u32[]{:S(2)}) collective-permute-start(bf16[1040,768]{1,0:T(8,128)(2,1)} %get-tuple-element.140), channel_id=1, source_target_pairs={{0,16},{8,24},{16,0},{24,8},{1,17},{9,25},{17,1},{25,9},{2,18},{10... | collective-permute-start | bytes 4792328 | tf_op jit(solution)/shard_map/ppermute | solution.py:26
  275.9 1.0 copy-start.12
  276.9 48.2 %collective-permute-start.31 = (bf16[1040,512]{1,0:T(8,128)(2,1)}, bf16[1040,512]{1,0:T(8,128)(2,1)S(1)}, u32[]{:S(2)}, u32[]{:S(2)}) collective-permute-start(bf16[1040,512]{1,0:T(8,128)(2,1)} %get-tuple-element.120), channel_id=1, source_target_pairs={{0,16},{8,24},{16,0},{24,8},{1,17},{9,25},{17,1},{25,9},{2,18},{10... | collective-permute-start | bytes 3194888 | tf_op jit(solution)/shard_map/ppermute | solution.py:26
  277.4 49.1 %collective-permute-start.33 = (bf16[1040,512]{1,0:T(8,128)(2,1)}, bf16[1040,512]{1,0:T(8,128)(2,1)S(1)}, u32[]{:S(2)}, u32[]{:S(2)}) collective-permute-start(bf16[1040,512]{1,0:T(8,128)(2,1)} %copy-done.12), channel_id=1, source_target_pairs={{0,8},{8,0},{16,24},{24,16},{1,9},{9,1},{17,25},{25,17},{2,10},{10... | collective-permute-start | bytes 3194888 | tf_op jit(solution)/shard_map/ppermute | solution.py:26
  278.1 1.2 copy-start.9
  279.3 1.0 copy-start.11
  303.8 32.1 %collective-permute-start.42 = (bf16[528,256]{1,0:T(8,128)(2,1)S(1)}, bf16[528,256]{1,0:T(8,128)(2,1)S(1)}, u32[]{:S(2)}, u32[]{:S(2)}) collective-permute-start(bf16[528,256]{1,0:T(8,128)(2,1)S(1)} %get-tuple-element.148), channel_id=1, source_target_pairs={{0,8},{8,0},{16,24},{24,16},{1,9},{9,1},{17,25},{25,17},{2,10},{10... | collective-permute-start | bytes 811016 | tf_op jit(solution)/shard_map/ppermute | solution.py:26
  304.4 29.9 %collective-permute-start.44 = (bf16[528,256]{1,0:T(8,128)(2,1)S(1)}, bf16[528,256]{1,0:T(8,128)(2,1)S(1)}, u32[]{:S(2)}, u32[]{:S(2)}) collective-permute-start(bf16[528,256]{1,0:T(8,128)(2,1)S(1)} %get-tuple-element.155), channel_id=1, source_target_pairs={{0,16},{8,24},{16,0},{24,8},{1,17},{9,25},{17,1},{25,9},{2,18},{10... | collective-permute-start | bytes 811016 | tf_op jit(solution)/shard_map/ppermute | solution.py:26
  325.0 17.4 %collective-permute-start.36 = (bf16[528,512]{1,0:T(8,128)(2,1)S(1)}, bf16[528,512]{1,0:T(8,128)(2,1)S(1)}, u32[]{:S(2)}, u32[]{:S(2)}) collective-permute-start(bf16[528,512]{1,0:T(8,128)(2,1)S(1)} %get-tuple-element.135), channel_id=1, source_target_pairs={{0,16},{8,24},{16,0},{24,8},{1,17},{9,25},{17,1},{25,9},{2,18},{10... | collective-permute-start | bytes 1622024 | tf_op jit(solution)/shard_map/ppermute | solution.py:26
  326.6 17.4 %collective-permute-start.34 = (bf16[528,512]{1,0:T(8,128)(2,1)S(1)}, bf16[528,512]{1,0:T(8,128)(2,1)S(1)}, u32[]{:S(2)}, u32[]{:S(2)}) collective-permute-start(bf16[528,512]{1,0:T(8,128)(2,1)S(1)} %get-tuple-element.128), channel_id=1, source_target_pairs={{0,8},{8,0},{16,24},{24,16},{1,9},{9,1},{17,25},{25,17},{2,10},{10... | collective-permute-start | bytes 1622024 | tf_op jit(solution)/shard_map/ppermute | solution.py:26
  334.3 25.5 %collective-permute-start.45 = (bf16[528,768]{1,0:T(8,128)(2,1)S(1)}, bf16[528,768]{1,0:T(8,128)(2,1)S(1)}, u32[]{:S(2)}, u32[]{:S(2)}) collective-permute-start(bf16[528,768]{1,0:T(8,128)(2,1)S(1)} %get-tuple-element.156), channel_id=1, source_target_pairs={{0,16},{8,24},{16,0},{24,8},{1,17},{9,25},{17,1},{25,9},{2,18},{10... | collective-permute-start | bytes 2433032 | tf_op jit(solution)/shard_map/ppermute | solution.py:26
  335.9 25.9 %collective-permute-start.43 = (bf16[528,768]{1,0:T(8,128)(2,1)S(1)}, bf16[528,768]{1,0:T(8,128)(2,1)S(1)}, u32[]{:S(2)}, u32[]{:S(2)}) collective-permute-start(bf16[528,768]{1,0:T(8,128)(2,1)S(1)} %get-tuple-element.149), channel_id=1, source_target_pairs={{0,8},{8,0},{16,24},{24,16},{1,9},{9,1},{17,25},{25,17},{2,10},{10... | collective-permute-start | bytes 2433032 | tf_op jit(solution)/shard_map/ppermute | solution.py:26
  342.4 25.5 %collective-permute-start.37 = (bf16[528,512]{1,0:T(8,128)(2,1)S(1)}, bf16[528,512]{1,0:T(8,128)(2,1)S(1)}, u32[]{:S(2)}, u32[]{:S(2)}) collective-permute-start(bf16[528,512]{1,0:T(8,128)(2,1)S(1)} %get-tuple-element.136), channel_id=1, source_target_pairs={{0,16},{8,24},{16,0},{24,8},{1,17},{9,25},{17,1},{25,9},{2,18},{10... | collective-permute-start | bytes 1622024 | tf_op jit(solution)/shard_map/ppermute | solution.py:26
  344.0 25.2 %collective-permute-start.35 = (bf16[528,512]{1,0:T(8,128)(2,1)S(1)}, bf16[528,512]{1,0:T(8,128)(2,1)S(1)}, u32[]{:S(2)}, u32[]{:S(2)}) collective-permute-start(bf16[528,512]{1,0:T(8,128)(2,1)S(1)} %get-tuple-element.129), channel_id=1, source_target_pairs={{0,8},{8,0},{16,24},{24,16},{1,9},{9,1},{17,25},{25,17},{2,10},{10... | collective-permute-start | bytes 1622024 | tf_op jit(solution)/shard_map/ppermute | solution.py:26
  (1 other events, 0.8 us)
Sparse Core Ops, SparseCore 0:
  61.2 48.6 all-gather.4
  111.5 45.8 all-gather.6
where the time goes:
time: 379 us; the launch traced here: 377 us
  waiting for transfers between devices  145 us (38%)
  Pallas kernels  108 us (28%)
  starting transfers between devices  52.7 us (14%)
  local copies, waits for them, and re-layouts  30.7 us (8%)
  other arithmetic  25.3 us (7%)
  between operations  15.7 us (4%)
    ppermute x46, waiting for transfers between devices, swap(): return lax.ppermute(value, axis, [(i, i ^ bits) for i in range(size)])  145 us
    ppermute x46, starting transfers between devices, swap(): return lax.ppermute(value, axis, [(i, i ^ bits) for i in range(size)])  52.6 us
    pallas_call x4, Pallas kernels, update_chunks(): pl.pallas_call(functools.partial(update_kernel, orders, steps), grid=(mem...  47.2 us
    pallas_call x6, Pallas kernels, gradient_chunk(): pl.pallas_call(functools.partial(gradient_kernel, dp, before is None), gr...  33.9 us
    pallas_call x8, Pallas kernels, fold_chunk(): pl.pallas_call(fold_kernel, grid=(width // tile,), in_specs=[spec(rows),...  16.4 us
    unnamed x36, local copies, waits for them, and re-layouts  15.5 us
    reduce_sum x1, other arithmetic, body(): weight_total = jnp.sum(jnp.sum(weight * weight, axis=0))  10.7 us
    pallas_call x8, Pallas kernels, hidden_chunk(): pl.pallas_call(hidden_kernel, grid=(width // tile,), in_specs=in_specs, o...  10.7 us
  transfers between devices with their start and end apart: 48, of which 22 were waited for; matrix products, arithmetic and copies ran while one was open for 11% of the time, Pallas kernels for 26%

commit v1 on v0

--- a/solution.py
+++ b/solution.py
@@ -84,7 +84,7 @@
 def gradient_kernel(dp, first, *refs):
     left = refs[0]
     blocks = refs[1 : 1 + dp]
-    gradient, rows, columns = refs[-3:]
+    gradient, rows, columns, short = refs[-4:]
     tokens = jnp.concatenate([block[...] for block in blocks], axis=0)
     total = []
     for i in range(left.shape[1]):
@@ -92,6 +92,7 @@
         total.append(jnp.dot(jnp.concatenate(pieces, axis=1), tokens, preferred_element_type=f32))
     total = jnp.concatenate(total, axis=0)
     gradient[...] = total
+    short[...] = total.astype(bf16)
     squares = total * total + tiny_square
     columns[...] = jnp.sum(squares, axis=0, keepdims=True)
     lanes = squares[:, 0:LANES]
@@ -124,10 +125,10 @@
         in_specs.append(shifted if n in near else apart)
     aliases = {}
     if before is not None:
-        gradient, row_part, column_part = before
-        aliases = {len(args) + 1: 0, len(args) + 2: 2}
-        args += [row_part, gradient, column_part]
-        in_specs += [whole((rows, LANES)), pl.BlockSpec(memory_space=pl.ANY), pl.BlockSpec(memory_space=pl.ANY)]
+        gradient, row_part, column_part, short = before
+        aliases = {len(args) + 1: 0, len(args) + 2: 2, len(args) + 3: 3}
+        args += [row_part, gradient, column_part, short]
+        in_specs += [whole((rows, LANES)), pl.BlockSpec(memory_space=pl.ANY), pl.BlockSpec(memory_space=pl.ANY), pl.BlockSpec(memory_space=pl.ANY)]
     return pl.pallas_call(
         functools.partial(gradient_kernel, dp, before is None),
         grid=(width // tile,),
@@ -136,11 +137,13 @@
             pl.BlockSpec((rows, tile), lambda j: (0, at + j)),
             whole((rows, LANES)),
             pl.BlockSpec((1, tile), lambda j: (0, at + j)),
+            pl.BlockSpec((rows, tile), lambda j: (0, at + j)),
         ],
         out_shape=[
             jax.ShapeDtypeStruct((rows, columns), f32),
             jax.ShapeDtypeStruct((rows, LANES), f32),
             jax.ShapeDtypeStruct((1, columns), f32),
+            jax.ShapeDtypeStruct((rows, columns), bf16),
         ],
         input_output_aliases=aliases,
         compiler_params=params(),
@@ -349,14 +352,15 @@
     for (start, width), blocks in zip(parts, far):
         near, offset = (near_ahead, 0) if start < edge else (near_behind, edge)
         before = gradient_chunk(left, out_grads, near, blocks, before, start, offset, width)
-    gradient, row_part, column_part = before
+    gradient, row_part, column_part, short = before
 
     row_sum = all_sum(jnp.sum(row_part, axis=1), "mp", mp)
     column_sum = all_sum(column_part[0], "dp", dp)
     row_moment = decay_rate * row_state + (1.0 - decay_rate) * (row_sum / (columns * mp))
     column_moment = decay_rate * column_state + (1.0 - decay_rate) * (column_sum / (rows * dp))
 
-    raw_columns = jnp.sum(gradient * gradient * (1.0 / row_moment)[:, None], axis=0)
+    short = short.astype(f32)
+    raw_columns = jnp.sum(short * short * (1.0 / row_moment)[:, None], axis=0)
     raw_total = jnp.sum(raw_columns / column_moment)
     totals = jnp.where(jnp.arange(LANES) == 0, raw_total, weight_total)
     totals = all_sum(all_sum(totals, "mp", mp), "dp", dp)

time: 379 us -> 384 us (1.013); the launches traced: 377 us -> 378 us
  transfers between devices with their start and end apart: 48 -> 48, of which waited for: 22 -> 22; matrix products, arithmetic and copies ran while one was open for 11% -> 10% of each run, Pallas kernels for 26% -> 27%
where the time goes in v1:
time: 384 us; the launch traced here: 378 us
  waiting for transfers between devices  145 us (38%)
  Pallas kernels  110 us (29%)
  starting transfers between devices  52.7 us (14%)
  local copies, waits for them, and re-layouts  30.7 us (8%)
  other arithmetic  24.1 us (6%)
  between operations  16.2 us (4%)
    ppermute x46, waiting for transfers between devices, swap(): return lax.ppermute(value, axis, [(i, i ^ bits) for i in range(size)])  145 us
    ppermute x46, starting transfers between devices, swap(): return lax.ppermute(value, axis, [(i, i ^ bits) for i in range(size)])  52.6 us
    pallas_call x4, Pallas kernels, update_chunks(): pl.pallas_call(functools.partial(update_kernel, orders, steps), grid=(mem...  47.4 us
    pallas_call x6, Pallas kernels, gradient_chunk(): pl.pallas_call(functools.partial(gradient_kernel, dp, before is None), gr...  35.4 us
    pallas_call x8, Pallas kernels, fold_chunk(): pl.pallas_call(fold_kernel, grid=(width // tile,), in_specs=[spec(rows),...  16.4 us
    unnamed x36, local copies, waits for them, and re-layouts  15.5 us
    reduce_sum x1, other arithmetic, body(): weight_total = jnp.sum(jnp.sum(weight * weight, axis=0))  10.7 us
    pallas_call x8, Pallas kernels, hidden_chunk(): pl.pallas_call(hidden_kernel, grid=(width // tile,), in_specs=in_specs, o...  10.7 us
  transfers between devices with their start and end apart: 48, of which 22 were waited for; matrix products, arithmetic and copies ran while one was open for 10% of the time, Pallas kernels for 27%

profile of v1, /device:TPU:0, one launch (start us, length us, event | category | flops | bytes accessed | tf_op | source)
XLA Modules:
  0.0 378.1 jit_solution(13907272191025201283)
XLA Ops:
  7.2 2.7 slice.36
  9.9 3.0 collective-permute-start.5
  12.8 1.5 collective-permute-start.4
  14.3 2.0 copy.45
  16.4 2.0 copy.46
  18.4 2.3 fusion.2
  20.7 1.6 collective-permute-start
  22.3 2.6 collective-permute-start.1
  25.1 8.0 %collective-permute-done = bf16[2,128,512]{1,2,0:T(8,128)(2,1)} collective-permute-done((bf16[2,128,512]{1,2,0:T(8,128)(2,1)}, bf16[2,128,512]{1,2,0:T(8,128)(2,1)}, u32[]{:S(2)}, u32[]{:S(2)}) %collective-permute-start) | collective-permute-done | bytes 262176 | tf_op jit(solution)/shard_map/ppermute | solution.py:26
  33.0 10.9 %collective-permute-done.1 = bf16[2,128,512]{1,2,0:T(8,128)(2,1)} collective-permute-done((bf16[2,128,512]{1,2,0:T(8,128)(2,1)}, bf16[2,128,512]{1,2,0:T(8,128)(2,1)}, u32[]{:S(2)}, u32[]{:S(2)}) %collective-permute-start.1) | collective-permute-done | bytes 262176 | tf_op jit(solution)/shard_map/ppermute | solution.py:26
  47.3 1.5 collective-permute-start.6
  48.8 1.7 slice.37
  50.5 5.4 %collective-permute-done.3 = bf16[2,128,512]{1,2,0:T(8,128)(2,1)S(1)} collective-permute-done((bf16[2,128,512]{1,2,0:T(8,128)(2,1)S(1)}, bf16[2,128,512]{1,2,0:T(8,128)(2,1)S(1)}, u32[]{:S(2)}, u32[]{:S(2)}) %collective-permute-start.3) | collective-permute-done | bytes 262176 | tf_op jit(solution)/shard_map/ppermute | solution.py:26
  56.0 3.9 %collective-permute-done.7 = bf16[2,128,512]{1,2,0:T(8,128)(2,1)S(1)} collective-permute-done((bf16[2,128,512]{1,2,0:T(8,128)(2,1)S(1)}, bf16[2,128,512]{1,2,0:T(8,128)(2,1)S(1)}, u32[]{:S(2)}, u32[]{:S(2)}) %collective-permute-start.7) | collective-permute-done | bytes 262176 | tf_op jit(solution)/shard_map/ppermute | solution.py:26
  61.2 2.1 copy.49
  63.3 1.8 collective-permute-start.9
  65.1 1.5 collective-permute-start.8
  66.6 2.1 slice.44
  68.7 2.2 slice.43
  71.6 10.7 %multiply_reduce_fusion.1 = f32[]{:T(128)} fusion(f32[1024,4096]{1,0:T(8,128)} %weight.7), kind=kLoop, calls=%fused_computation.1 | loop fusion | flops 8388607 | bytes 16777220 | tf_op jit(solution)/shard_map/reduce_sum | solution.py:337
  82.3 41.0 %collective-permute-done.9.refs_3_ = bf16[512,2560]{1,0:T(8,128)(2,1)S(1)} collective-permute-done((bf16[512,2560]{1,0:T(8,128)(2,1)}, bf16[512,2560]{1,0:T(8,128)(2,1)S(1)}, u32[]{:S(2)}, u32[]{:S(2)}) %collective-permute-start.9) | collective-permute-done | bytes 2621472 | tf_op jit(solution)/shard_map/ppermute | solution.py:26
  123.3 1.8 collective-permute-done.8.refs_2_
  126.9 1.8 collective-permute-start.12
  129.8 1.6 collective-permute-start.11
  131.5 8.7 %collective-permute-done.15.refs_4_ = bf16[512,768]{1,0:T(8,128)(2,1)S(1)} collective-permute-done((bf16[512,768]{1,0:T(8,128)(2,1)}, bf16[512,768]{1,0:T(8,128)(2,1)S(1)}, u32[]{:S(2)}, u32[]{:S(2)}) %collective-permute-start.15) | collective-permute-done | bytes 786464 | tf_op jit(solution)/shard_map/ppermute | solution.py:26
  140.2 1.7 collective-permute-start.10
  141.9 2.3 copy-done.2
  147.0 5.9 %gradient_chunk.6 = (f32[1024,4096]{1,0:T(8,128)}, f32[1024,128]{1,0:T(8,128)S(1)}, f32[1,4096]{1,0:T(1,128)S(1)}, bf16[1024,4096]{1,0:T(8,128)(2,1)}) custom-call(bf16[4,2,4,512,128]{4,3,2,1,0:T(8,128)(2,1)S(1)} %bitcast.31, bf16[512,4096]{1,0:T(8,128)(2,1)S(1)} %copy-done.1, bf16[512,1536]{1,0:T(8,128)(2,1)S(1)} %copy-done.7, ...), custom_call_target="tpu_custom_call" | custom-call | flops 32212254 | bytes 104857 | tf_op jit(solution)/shard_map/gradient_chunk/pallas_call | solution.py:132
  152.9 6.5 %gradient_chunk.7 = (f32[1024,4096]{1,0:T(8,128)}, f32[1024,128]{1,0:T(8,128)S(1)}, f32[1,4096]{1,0:T(1,128)S(1)}, bf16[1024,4096]{1,0:T(8,128)(2,1)}) custom-call(bf16[4,2,4,512,128]{4,3,2,1,0:T(8,128)(2,1)S(1)} %bitcast.32, bf16[512,4096]{1,0:T(8,128)(2,1)S(1)} %copy-done.1, ...), custom_call_target="tpu_custom_call", output_to_operand_aliasing={{0}: (6, {}), {2}: (7, {}), {3}: (8, {})} | custom-call | flops 32212254 | bytes 104857 | tf_op jit(solution)/shard_map/gradient_chunk/pallas_call | solution.py:132
  159.4 6.5 %gradient_chunk.8 = (f32[1024,4096]{1,0:T(8,128)}, f32[1024,128]{1,0:T(8,128)S(1)}, f32[1,4096]{1,0:T(1,128)S(1)}, bf16[1024,4096]{1,0:T(8,128)(2,1)}) custom-call(bf16[4,2,4,512,128]{4,3,2,1,0:T(8,128)(2,1)S(1)} %bitcast.33, bf16[512,4096]{1,0:T(8,128)(2,1)S(1)} %copy-done.1, ...), custom_call_target="tpu_custom_call", output_to_operand_aliasing={{0}: (6, {}), {2}: (7, {}), {3}: (8, {})} | custom-call | flops 32212254 | bytes 104857 | tf_op jit(solution)/shard_map/gradient_chunk/pallas_call | solution.py:132
  166.0 6.5 %gradient_chunk.9 = (f32[1024,4096]{1,0:T(8,128)}, f32[1024,128]{1,0:T(8,128)S(1)}, f32[1,4096]{1,0:T(1,128)S(1)}, bf16[1024,4096]{1,0:T(8,128)(2,1)}) custom-call(bf16[4,2,4,512,128]{4,3,2,1,0:T(8,128)(2,1)S(1)} %bitcast.34, bf16[512,4096]{1,0:T(8,128)(2,1)S(1)} %copy-done.1, ...), custom_call_target="tpu_custom_call", output_to_operand_aliasing={{0}: (6, {}), {2}: (7, {}), {3}: (8, {})} | custom-call | flops 32212254 | bytes 104857 | tf_op jit(solution)/shard_map/gradient_chunk/pallas_call | solution.py:132
  172.5 5.0 %gradient_chunk.10 = (f32[1024,4096]{1,0:T(8,128)}, f32[1024,128]{1,0:T(8,128)S(1)}, f32[1,4096]{1,0:T(1,128)S(1)}, bf16[1024,4096]{1,0:T(8,128)(2,1)}) custom-call(bf16[4,2,4,512,128]{4,3,2,1,0:T(8,128)(2,1)S(1)} %bitcast.35, bf16[512,4096]{1,0:T(8,128)(2,1)S(1)} %copy-done.1, ...), custom_call_target="tpu_custom_call", output_to_operand_aliasing={{0}: (6, {}), {2}: (7, {}), {3}: (8, {})} | custom-call | flops 21474836 | bytes 83886 | tf_op jit(solution)/shard_map/gradient_chunk/pallas_call | solution.py:132
  177.5 5.0 %gradient_chunk.11 = (f32[1024,4096]{1,0:T(8,128)}, f32[1024,128]{1,0:T(8,128)S(1)}, f32[1,4096]{1,0:T(1,128)S(1)}, bf16[1024,4096]{1,0:T(8,128)(2,1)}) custom-call(bf16[4,2,4,512,128]{4,3,2,1,0:T(8,128)(2,1)S(1)} %bitcast.36, bf16[512,4096]{1,0:T(8,128)(2,1)S(1)} %copy-done.1, ...), custom_call_target="tpu_custom_call", output_to_operand_aliasing={{0}: (6, {}), {2}: (7, {}), {3}: (8, {})} | custom-call | flops 21474836 | bytes 83886 | tf_op jit(solution)/shard_map/gradient_chunk/pallas_call | solution.py:132
  182.8 2.5 collective-permute-start.17
  186.9 3.1 collective-permute-start.19
  190.0 1.7 collective-permute-start.22
  193.5 6.4 %multiply_reduce_fusion = f32[4096]{0:T(1024)S(1)} fusion(bf16[1024,4096]{1,0:T(8,128)(2,1)} %get-tuple-element.116, f32[1024]{0:T(1024)S(1)} %broadcast_divide_fusion), kind=kLoop, calls=%fused_computation | loop fusion | flops 16773120 | bytes 8409088 | tf_op jit(solution)/shard_map/reduce_sum | solution.py:363
  202.6 1.5 collective-permute-start.23
  208.0 3.2 collective-permute-done.26
  211.3 1.6 collective-permute-start.29
  219.0 2.2 copy-done.3
  221.2 7.2 %update_chunks.4 = (f32[1024,4096]{1,0:T(8,128)}, f32[1024,4096]{1,0:T(8,128)}, bf16[1040,256]{1,0:T(8,128)(2,1)S(1)}, bf16[1040,256]{1,0:T(8,128)(2,1)S(1)}, f3...) custom-call(f32[1,1]{1,0:T(1,128)} %bitcast.18.step, f32[1024,4096]{1,0:T(8,128)} %get-tuple-element.120.gradient, ...), custom_call_target="tpu_custom_call" | custom-call | flops 21474836 | bytes 157286 | tf_op jit(solution)/shard_map/update_chunks/pallas_call | solution.py:208
  228.4 1.6 collective-permute-start.38
  231.2 11.7 %update_chunks.5 = (f32[1024,4096]{1,0:T(8,128)}, f32[1024,4096]{1,0:T(8,128)}, bf16[1040,512]{1,0:T(8,128)(2,1)S(1)}, bf16[1040,512]{1,0:T(8,128)(2,1)}, f32[10...) custom-call(f32[1,1]{1,0:T(1,128)} %bitcast.18.step, ...), custom_call_target="tpu_custom_call", output_to_operand_aliasing={{0}: (6, {}), {1}: (7, {})} | custom-call | flops 42949672 | bytes 272629 | tf_op jit(solution)/shard_map/update_chunks/pallas_call | solution.py:208
  244.2 16.7 %update_chunks.6 = (f32[1024,4096]{1,0:T(8,128)}, f32[1024,4096]{1,0:T(8,128)}, bf16[1040,768]{1,0:T(8,128)(2,1)}, bf16[1040,768]{1,0:T(8,128)(2,1)}, f32[1024,768]{1,0:T(8,128)S(1)}, /*index=5*/f32[1024,768]{1,0:T(8,128)S(1)}) custom-call(f32[1,1]{1,0:T(1,128)} %bitcast.18.step, ...), custom_call_target="tpu_custom_call", output_to_operand_aliasing={{0}: (6, {}), {1}: (7, {})} | custom-call | flops 64424508 | bytes 387973 | tf_op jit(solution)/shard_map/update_chunks/pallas_call | solution.py:208
  263.1 1.4 collective-permute-start.39
  264.6 11.7 %update_chunks.7 = (f32[1024,4096]{1,0:T(8,128)}, f32[1024,4096]{1,0:T(8,128)}, bf16[1040,512]{1,0:T(8,128)(2,1)S(1)}, bf16[1040,512]{1,0:T(8,128)(2,1)}, f32[10...) custom-call(f32[1,1]{1,0:T(1,128)} %bitcast.18.step, ...), custom_call_target="tpu_custom_call", output_to_operand_aliasing={{0}: (6, {}), {1}: (7, {})} | custom-call | flops 42949672 | bytes 272629 | tf_op jit(solution)/shard_map/update_chunks/pallas_call | solution.py:208
  282.5 1.9 fold_chunk.9
  284.4 2.2 fold_chunk.11
  286.6 17.6 %collective-permute-done.41.arrived = bf16[1040,768]{1,0:T(8,128)(2,1)S(1)} collective-permute-done((bf16[1040,768]{1,0:T(8,128)(2,1)}, bf16[1040,768]{1,0:T(8,128)(2,1)S(1)}, u32[]{:S(2)}, u32[]{:S(2)}) %collective-permute-start.41) | collective-permute-done | bytes 1597472 | tf_op jit(solution)/shard_map/ppermute | solution.py:26
  304.8 1.5 collective-permute-start.44
  306.3 19.2 %collective-permute-done.31.arrived = bf16[1040,512]{1,0:T(8,128)(2,1)S(1)} collective-permute-done((bf16[1040,512]{1,0:T(8,128)(2,1)}, bf16[1040,512]{1,0:T(8,128)(2,1)S(1)}, u32[]{:S(2)}, u32[]{:S(2)}) %collective-permute-start.31) | collective-permute-done | bytes 1064992 | tf_op jit(solution)/shard_map/ppermute | solution.py:26
  325.5 1.5 collective-permute-done.33.arrived
  327.6 2.9 fold_chunk.14
  330.5 3.9 %fold_chunk.12 = (bf16[528,768]{1,0:T(8,128)(2,1)S(1)}, f32[512,768]{1,0:T(8,128)S(1)}) custom-call(f32[1024,768]{1,0:T(8,128)S(1)} %get-tuple-element.149.kept, bf16[1040,768]{1,0:T(8,128)(2,1)} %collective-permute-done.39.arrived), custom_call_target="tpu_custom_call" | custom-call | flops 157286 | bytes 70778 | tf_op jit(solution)/shard_map/fold_chunk/pallas_call | solution.py:242
  334.5 1.6 collective-permute-start.45
  337.4 1.9 fold_chunk.10
  339.3 1.9 fold_chunk.8
  341.3 1.6 collective-permute-done.36.arrived
  342.9 1.5 collective-permute-done.34.arrived
  349.3 10.9 %collective-permute-done.45.arrived = bf16[528,768]{1,0:T(8,128)(2,1)S(1)} collective-permute-done((bf16[528,768]{1,0:T(8,128)(2,1)S(1)}, bf16[528,768]{1,0:T(8,128)(2,1)S(1)}, u32[]{:S(2)}, u32[]{:S(2)}) %collective-permute-start.45) | collective-permute-done | bytes 811040 | tf_op jit(solution)/shard_map/ppermute | solution.py:26
  360.3 1.9 hidden_chunk.12.refs_0_
  362.2 1.9 hidden_chunk.13.refs_0_
  364.1 4.2 %collective-permute-done.37.arrived = bf16[528,512]{1,0:T(8,128)(2,1)S(1)} collective-permute-done((bf16[528,512]{1,0:T(8,128)(2,1)S(1)}, bf16[528,512]{1,0:T(8,128)(2,1)S(1)}, u32[]{:S(2)}, u32[]{:S(2)}) %collective-permute-start.37) | collective-permute-done | bytes 540704 | tf_op jit(solution)/shard_map/ppermute | solution.py:26
  (124 shorter events, 47.2 us)
Async XLA Ops:
  7.2 118.0 %all-gather.5.cloned.1.call-start = ((), (), s32[]{:S(2)}) async-start(), calls=%async_computation | async-start | bytes 4718592 | tf_op jit(solution)/shard_map/all_gather | solution.py:296
  9.9 46.1 %collective-permute-start.5 = (bf16[512,1536]{1,0:T(8,128)(2,1)}, bf16[512,1536]{1,0:T(8,128)(2,1)S(1)}, u32[]{:S(2)}, u32[]{:S(2)}) collective-permute-start(bf16[512,1536]{1,0:T(8,128)(2,1)} %slice.36), channel_id=1, source_target_pairs={{0,16},{8,24},{16,0},{24,8},{1,17},{9,25},{17,1},{25,9},{2,18},{10... | collective-permute-start | bytes 4718600 | tf_op jit(solution)/shard_map/ppermute | solution.py:26
  12.8 43.2 %collective-permute-start.4 = (bf16[512,1536]{1,0:T(8,128)(2,1)}, bf16[512,1536]{1,0:T(8,128)(2,1)S(1)}, u32[]{:S(2)}, u32[]{:S(2)}) collective-permute-start(bf16[512,1536]{1,0:T(8,128)(2,1)} %slice.36), channel_id=1, source_target_pairs={{0,8},{8,0},{16,24},{24,16},{1,9},{9,1},{17,25},{25,17},{2,10},{10... | collective-permute-start | bytes 4718600 | tf_op jit(solution)/shard_map/ppermute | solution.py:26
  20.7 12.4 %collective-permute-start = (bf16[2,128,512]{1,2,0:T(8,128)(2,1)}, bf16[2,128,512]{1,2,0:T(8,128)(2,1)}, u32[]{:S(2)}, u32[]{:S(2)}) collective-permute-start(bf16[2,128,512]{1,2,0:T(8,128)(2,1)} %get-tuple-element.184), channel_id=1, source_target_pairs={{0,2},{1,3},{2,0},{3,1},{4,6},{5,7},{6,4},{7,5},{8,10},{9,11},{10,... | collective-permute-start | bytes 786440 | tf_op jit(solution)/shard_map/ppermute | solution.py:26
  22.3 21.7 %collective-permute-start.1 = (bf16[2,128,512]{1,2,0:T(8,128)(2,1)}, bf16[2,128,512]{1,2,0:T(8,128)(2,1)}, u32[]{:S(2)}, u32[]{:S(2)}) collective-permute-start(bf16[2,128,512]{1,2,0:T(8,128)(2,1)} %get-tuple-element.185), channel_id=1, source_target_pairs={{0,4},{1,5},{2,6},{3,7},{4,0},{5,1},{6,2},{7,3},{8,12},{9,13},{10,... | collective-permute-start | bytes 786440 | tf_op jit(solution)/shard_map/ppermute | solution.py:26
  24.8 19.1 %collective-permute-start.2 = (bf16[2,128,512]{1,2,0:T(8,128)(2,1)}, bf16[2,128,512]{1,2,0:T(8,128)(2,1)}, u32[]{:S(2)}, u32[]{:S(2)}) collective-permute-start(bf16[2,128,512]{1,2,0:T(8,128)(2,1)} %get-tuple-element.186), channel_id=1, source_target_pairs={{0,6},{1,7},{2,4},{3,5},{4,2},{5,3},{6,0},{7,1},{8,14},{9,15},{10,... | collective-permute-start | bytes 786440 | tf_op jit(solution)/shard_map/ppermute | solution.py:26
  25.1 23.8 %copy-start = (bf16[512,4096]{1,0:T(8,128)(2,1)S(1)}, bf16[512,4096]{1,0:T(8,128)(2,1)}, u32[]{:S(2)}) copy-start(bf16[512,4096]{1,0:T(8,128)(2,1)} %refs_1_.11) | copy-start | bytes 12582916
  45.3 10.7 %collective-permute-start.3 = (bf16[2,128,512]{1,2,0:T(8,128)(2,1)S(1)}, bf16[2,128,512]{1,2,0:T(8,128)(2,1)S(1)}, u32[]{:S(2)}, u32[]{:S(2)}) collective-permute-start(bf16[2,128,512]{1,2,0:T(8,128)(2,1)S(1)} %get-tuple-element.182), channel_id=1, source_target_pairs={{0,8},{8,0},{16,24},{24,16},{1,9},{9,1},{17,25},{25,17},{2,10},{10... | collective-permute-start | bytes 786440 | tf_op jit(solution)/shard_map/ppermute | solution.py:26
  45.9 14.0 %collective-permute-start.7 = (bf16[2,128,512]{1,2,0:T(8,128)(2,1)S(1)}, bf16[2,128,512]{1,2,0:T(8,128)(2,1)S(1)}, u32[]{:S(2)}, u32[]{:S(2)}) collective-permute-start(bf16[2,128,512]{1,2,0:T(8,128)(2,1)S(1)} %get-tuple-element.180), channel_id=1, source_target_pairs={{0,24},{8,16},{16,8},{24,0},{1,25},{9,17},{17,9},{25,1},{2,26},{10... | collective-permute-start | bytes 786440 | tf_op jit(solution)/shard_map/ppermute | solution.py:26
  47.3 12.5 %collective-permute-start.6 = (bf16[2,128,512]{1,2,0:T(8,128)(2,1)S(1)}, bf16[2,128,512]{1,2,0:T(8,128)(2,1)S(1)}, u32[]{:S(2)}, u32[]{:S(2)}) collective-permute-start(bf16[2,128,512]{1,2,0:T(8,128)(2,1)S(1)} %get-tuple-element.181), channel_id=1, source_target_pairs={{0,16},{8,24},{16,0},{24,8},{1,17},{9,25},{17,1},{25,9},{2,18},{10... | collective-permute-start | bytes 786440 | tf_op jit(solution)/shard_map/ppermute | solution.py:26
  56.0 7.3 %copy-start.4 = (bf16[512,1536]{1,0:T(8,128)(2,1)}, bf16[512,1536]{1,0:T(8,128)(2,1)S(1)}, u32[]{:S(2)}) copy-start(bf16[512,1536]{1,0:T(8,128)(2,1)S(1)} %collective-permute-done.5.refs_3_) | copy-start | bytes 4718596
  56.0 7.3 %copy-start.6 = (bf16[512,1536]{1,0:T(8,128)(2,1)}, bf16[512,1536]{1,0:T(8,128)(2,1)S(1)}, u32[]{:S(2)}) copy-start(bf16[512,1536]{1,0:T(8,128)(2,1)S(1)} %collective-permute-done.4.refs_2_) | copy-start | bytes 4718596
  61.1 157.8 %all-gather.7.cloned.1.call-start = ((), (), s32[]{:S(2)}) async-start(), calls=%async_computation.1 | async-start | bytes 4718592 | tf_op jit(solution)/shard_map/all_gather | solution.py:296
  63.3 60.1 %collective-permute-start.9 = (bf16[512,2560]{1,0:T(8,128)(2,1)}, bf16[512,2560]{1,0:T(8,128)(2,1)S(1)}, u32[]{:S(2)}, u32[]{:S(2)}) collective-permute-start(bf16[512,2560]{1,0:T(8,128)(2,1)} %slice.37), channel_id=1, source_target_pairs={{0,16},{8,24},{16,0},{24,8},{1,17},{9,25},{17,1},{25,9},{2,18},{10... | collective-permute-start | bytes 7864328 | tf_op jit(solution)/shard_map/ppermute | solution.py:26
  65.1 60.1 %collective-permute-start.8 = (bf16[512,2560]{1,0:T(8,128)(2,1)}, bf16[512,2560]{1,0:T(8,128)(2,1)}, u32[]{:S(2)}, u32[]{:S(2)}) collective-permute-start(bf16[512,2560]{1,0:T(8,128)(2,1)} %slice.37), channel_id=1, source_target_pairs={{0,8},{8,0},{16,24},{24,16},{1,9},{9,1},{17,25},{25,17},{2,10},{10... | collective-permute-start | bytes 7864328 | tf_op jit(solution)/shard_map/ppermute | solution.py:26
  70.8 82.1 %collective-permute-start.14 = (bf16[512,768]{1,0:T(8,128)(2,1)}, bf16[512,768]{1,0:T(8,128)(2,1)}, u32[]{:S(2)}, u32[]{:S(2)}) collective-permute-start(bf16[512,768]{1,0:T(8,128)(2,1)} %slice.43), channel_id=1, source_target_pairs={{0,8},{8,0},{16,24},{24,16},{1,9},{9,1},{17,25},{25,17},{2,10},{10... | collective-permute-start | bytes 2359304 | tf_op jit(solution)/shard_map/ppermute | solution.py:26
  71.3 68.9 %collective-permute-start.15 = (bf16[512,768]{1,0:T(8,128)(2,1)}, bf16[512,768]{1,0:T(8,128)(2,1)S(1)}, u32[]{:S(2)}, u32[]{:S(2)}) collective-permute-start(bf16[512,768]{1,0:T(8,128)(2,1)} %slice.44), channel_id=1, source_target_pairs={{0,16},{8,24},{16,0},{24,8},{1,17},{9,25},{17,1},{25,9},{2,18},{10... | collective-permute-start | bytes 2359304 | tf_op jit(solution)/shard_map/ppermute | solution.py:26
  125.2 16.7 %copy-start.1 = (bf16[512,4096]{1,0:T(8,128)(2,1)S(1)}, bf16[512,4096]{1,0:T(8,128)(2,1)}, u32[]{:S(2)}) copy-start(bf16[512,4096]{1,0:T(8,128)(2,1)} %refs_1_.11) | copy-start | bytes 12582916
  126.6 32.9 %collective-permute-start.13 = (bf16[512,768]{1,0:T(8,128)(2,1)S(1)}, bf16[512,768]{1,0:T(8,128)(2,1)S(1)}, u32[]{:S(2)}, u32[]{:S(2)}) collective-permute-start(bf16[512,768]{1,0:T(8,128)(2,1)S(1)} %slice.42), channel_id=1, source_target_pairs={{0,16},{8,24},{16,0},{24,8},{1,17},{9,25},{17,1},{25,9},{2,18},{10... | collective-permute-start | bytes 2359304 | tf_op jit(solution)/shard_map/ppermute | solution.py:26
  126.9 39.0 %collective-permute-start.12 = (bf16[512,768]{1,0:T(8,128)(2,1)S(1)}, bf16[512,768]{1,0:T(8,128)(2,1)S(1)}, u32[]{:S(2)}, u32[]{:S(2)}) collective-permute-start(bf16[512,768]{1,0:T(8,128)(2,1)S(1)} %slice.41), channel_id=1, source_target_pairs={{0,8},{8,0},{16,24},{24,16},{1,9},{9,1},{17,25},{25,17},{2,10},{10... | collective-permute-start | bytes 2359304 | tf_op jit(solution)/shard_map/ppermute | solution.py:26
  129.8 42.7 %collective-permute-start.11 = (bf16[512,512]{1,0:T(8,128)(2,1)S(1)}, bf16[512,512]{1,0:T(8,128)(2,1)S(1)}, u32[]{:S(2)}, u32[]{:S(2)}) collective-permute-start(bf16[512,512]{1,0:T(8,128)(2,1)S(1)} %slice.40), channel_id=1, source_target_pairs={{0,16},{8,24},{16,0},{24,8},{1,17},{9,25},{17,1},{25,9},{2,18},{10... | collective-permute-start | bytes 1572872 | tf_op jit(solution)/shard_map/ppermute | solution.py:26
  140.2 37.3 %collective-permute-start.10 = (bf16[512,512]{1,0:T(8,128)(2,1)S(1)}, bf16[512,512]{1,0:T(8,128)(2,1)S(1)}, u32[]{:S(2)}, u32[]{:S(2)}) collective-permute-start(bf16[512,512]{1,0:T(8,128)(2,1)S(1)} %slice.39), channel_id=1, source_target_pairs={{0,8},{8,0},{16,24},{24,16},{1,9},{9,1},{17,25},{25,17},{2,10},{10... | collective-permute-start | bytes 1572872 | tf_op jit(solution)/shard_map/ppermute | solution.py:26
  141.9 2.3 copy-start.2
  144.2 1.4 copy-start.5
  145.6 1.4 copy-start.7
  177.5 16.0 %copy-start.16 = (f32[1024]{0:T(1024)S(1)}, f32[1024]{0:T(1024)}, u32[]{:S(2)}) copy-start(f32[1024]{0:T(1024)} %param.9) | copy-start | bytes 12292
  182.7 3.1 collective-permute-start.18
  182.8 4.1 %collective-permute-start.17 = (f32[1024]{0:T(1024)S(1)}, f32[1024]{0:T(1024)S(1)}, u32[]{:S(2)}, u32[]{:S(2)}) collective-permute-start(f32[1024]{0:T(1024)S(1)} %reduce_sum.41), channel_id=1, source_target_pairs={{0,2},{1,3},{2,0},{3,1},{4,6},{5,7},{6,4},{7,5},{8,10},{9,11},{10,... | collective-permute-start | bytes 12296 | tf_op jit(solution)/shard_map/ppermute | solution.py:26
  185.3 1.6 collective-permute-start.16
  186.9 6.6 %collective-permute-start.19 = (f32[1024]{0:T(1024)S(1)}, f32[1024]{0:T(1024)S(1)}, u32[]{:S(2)}, u32[]{:S(2)}) collective-permute-start(f32[1024]{0:T(1024)S(1)} %add_add_fusion), channel_id=1, source_target_pairs={{0,4},{1,5},{2,6},{3,7},{4,0},{5,1},{6,2},{7,3},{8,12},{9,13},{10,... | collective-permute-start | bytes 12296 | tf_op jit(solution)/shard_map/ppermute | solution.py:26
  190.0 10.0 %collective-permute-start.22 = (f32[4096]{0:T(1024)S(1)}, f32[4096]{0:T(1024)S(1)}, u32[]{:S(2)}, u32[]{:S(2)}) collective-permute-start(f32[4096]{0:T(1024)S(1)} %bitcast.41), channel_id=1, source_target_pairs={{0,24},{8,16},{16,8},{24,0},{1,25},{9,17},{17,9},{25,1},{2,26},{10... | collective-permute-start | bytes 49160 | tf_op jit(solution)/shard_map/ppermute | solution.py:26
  191.7 8.3 %collective-permute-start.21 = (f32[4096]{0:T(1024)S(1)}, f32[4096]{0:T(1024)S(1)}, u32[]{:S(2)}, u32[]{:S(2)}) collective-permute-start(f32[4096]{0:T(1024)S(1)} %bitcast.42), channel_id=1, source_target_pairs={{0,16},{8,24},{16,0},{24,8},{1,17},{9,25},{17,1},{25,9},{2,18},{10... | collective-permute-start | bytes 49160 | tf_op jit(solution)/shard_map/ppermute | solution.py:26
  192.2 7.8 %collective-permute-start.20 = (f32[4096]{0:T(1024)S(1)}, f32[4096]{0:T(1024)S(1)}, u32[]{:S(2)}, u32[]{:S(2)}) collective-permute-start(f32[4096]{0:T(1024)S(1)} %bitcast.43), channel_id=1, source_target_pairs={{0,8},{8,0},{16,24},{24,16},{1,9},{9,1},{17,25},{25,17},{2,10},{10... | collective-permute-start | bytes 49160 | tf_op jit(solution)/shard_map/ppermute | solution.py:26
  193.5 6.5 %copy-start.15 = (f32[1024]{0:T(1024)}, f32[1024]{0:T(1024)S(1)}, u32[]{:S(2)}) copy-start(f32[1024]{0:T(1024)S(1)} %get-tuple-element.174) | copy-start | bytes 12292
  193.5 6.5 %copy-start.14 = (f32[4096]{0:T(1024)S(1)}, f32[4096]{0:T(1024)}, u32[]{:S(2)}) copy-start(f32[4096]{0:T(1024)} %param.10) | copy-start | bytes 49156
  200.6 27.8 %copy-start.13 = (f32[4096]{0:T(1024)}, f32[4096]{0:T(1024)S(1)}, u32[]{:S(2)}) copy-start(f32[4096]{0:T(1024)S(1)} %get-tuple-element.176) | copy-start | bytes 49156
  201.8 3.6 collective-permute-start.24
  202.6 3.0 collective-permute-start.25
  202.6 3.0 collective-permute-start.23
  206.8 4.5 %collective-permute-start.26 = (f32[128]{0:T(128)S(1)}, f32[128]{0:T(128)S(1)}, u32[]{:S(2)}, u32[]{:S(2)}) collective-permute-start(f32[128]{0:T(128)S(1)} %add_add_fusion.2), channel_id=1, source_target_pairs={{0,4},{1,5},{2,6},{3,7},{4,0},{5,1},{6,2},{7,3},{8,12},{9,13},{10,... | collective-permute-start | bytes 1544 | tf_op jit(solution)/shard_map/ppermute | solution.py:26
  211.3 4.4 %collective-permute-start.29 = (f32[128]{0:T(128)S(1)}, f32[128]{0:T(128)S(1)}, u32[]{:S(2)}, u32[]{:S(2)}) collective-permute-start(f32[128]{0:T(128)S(1)} %add.98), channel_id=1, source_target_pairs={{0,24},{8,16},{16,8},{24,0},{1,25},{9,17},{17,9},{25,1},{2,26},{10... | collective-permute-start | bytes 1544 | tf_op jit(solution)/shard_map/ppermute | solution.py:26
  212.9 3.5 collective-permute-start.28
  213.4 3.5 collective-permute-start.27
  219.0 2.2 copy-start.3
  228.4 14.6 %copy-start.8 = (f32[1024,256]{1,0:T(8,128)}, f32[1024,256]{1,0:T(8,128)S(1)}, u32[]{:S(2)}) copy-start(f32[1024,256]{1,0:T(8,128)S(1)} %get-tuple-element.155.kept) | copy-start | bytes 3145732
  228.4 34.0 %collective-permute-start.38 = (bf16[1040,256]{1,0:T(8,128)(2,1)S(1)}, bf16[1040,256]{1,0:T(8,128)(2,1)S(1)}, u32[]{:S(2)}, u32[]{:S(2)}) collective-permute-start(bf16[1040,256]{1,0:T(8,128)(2,1)S(1)} %get-tuple-element.151), channel_id=1, source_target_pairs={{0,16},{8,24},{16,0},{24,8},{1,17},{9,25},{17,1},{25,9},{2,18},{10... | collective-permute-start | bytes 1597448 | tf_op jit(solution)/shard_map/ppermute | solution.py:26
  230.0 31.0 %collective-permute-start.40 = (bf16[1040,256]{1,0:T(8,128)(2,1)S(1)}, bf16[1040,256]{1,0:T(8,128)(2,1)S(1)}, u32[]{:S(2)}, u32[]{:S(2)}) collective-permute-start(bf16[1040,256]{1,0:T(8,128)(2,1)S(1)} %get-tuple-element.158), channel_id=1, source_target_pairs={{0,8},{8,0},{16,24},{24,16},{1,9},{9,1},{17,25},{25,17},{2,10},{10... | collective-permute-start | bytes 1597448 | tf_op jit(solution)/shard_map/ppermute | solution.py:26
  243.0 34.4 %collective-permute-start.30 = (bf16[1040,512]{1,0:T(8,128)(2,1)}, bf16[1040,512]{1,0:T(8,128)(2,1)S(1)}, u32[]{:S(2)}, u32[]{:S(2)}) collective-permute-start(bf16[1040,512]{1,0:T(8,128)(2,1)} %get-tuple-element.131), channel_id=1, source_target_pairs={{0,16},{8,24},{16,0},{24,8},{1,17},{9,25},{17,1},{25,9},{2,18},{10... | collective-permute-start | bytes 3194888 | tf_op jit(solution)/shard_map/ppermute | solution.py:26
  243.5 34.4 %collective-permute-start.32 = (bf16[1040,512]{1,0:T(8,128)(2,1)S(1)}, bf16[1040,512]{1,0:T(8,128)(2,1)S(1)}, u32[]{:S(2)}, u32[]{:S(2)}) collective-permute-start(bf16[1040,512]{1,0:T(8,128)(2,1)S(1)} %get-tuple-element.138), channel_id=1, source_target_pairs={{0,8},{8,0},{16,24},{24,16},{1,9},{9,1},{17,25},{25,17},{2,10},{10... | collective-permute-start | bytes 3194888 | tf_op jit(solution)/shard_map/ppermute | solution.py:26
  260.9 43.3 %collective-permute-start.41 = (bf16[1040,768]{1,0:T(8,128)(2,1)}, bf16[1040,768]{1,0:T(8,128)(2,1)S(1)}, u32[]{:S(2)}, u32[]{:S(2)}) collective-permute-start(bf16[1040,768]{1,0:T(8,128)(2,1)} %get-tuple-element.159), channel_id=1, source_target_pairs={{0,8},{8,0},{16,24},{24,16},{1,9},{9,1},{17,25},{25,17},{2,10},{10... | collective-permute-start | bytes 4792328 | tf_op jit(solution)/shard_map/ppermute | solution.py:26
  263.1 41.7 %collective-permute-start.39 = (bf16[1040,768]{1,0:T(8,128)(2,1)}, bf16[1040,768]{1,0:T(8,128)(2,1)}, u32[]{:S(2)}, u32[]{:S(2)}) collective-permute-start(bf16[1040,768]{1,0:T(8,128)(2,1)} %get-tuple-element.152), channel_id=1, source_target_pairs={{0,16},{8,24},{16,0},{24,8},{1,17},{9,25},{17,1},{25,9},{2,18},{10... | collective-permute-start | bytes 4792328 | tf_op jit(solution)/shard_map/ppermute | solution.py:26
  276.3 1.0 copy-start.12
  277.3 48.2 %collective-permute-start.31 = (bf16[1040,512]{1,0:T(8,128)(2,1)}, bf16[1040,512]{1,0:T(8,128)(2,1)S(1)}, u32[]{:S(2)}, u32[]{:S(2)}) collective-permute-start(bf16[1040,512]{1,0:T(8,128)(2,1)} %get-tuple-element.132), channel_id=1, source_target_pairs={{0,16},{8,24},{16,0},{24,8},{1,17},{9,25},{17,1},{25,9},{2,18},{10... | collective-permute-start | bytes 3194888 | tf_op jit(solution)/shard_map/ppermute | solution.py:26
  277.9 49.1 %collective-permute-start.33 = (bf16[1040,512]{1,0:T(8,128)(2,1)}, bf16[1040,512]{1,0:T(8,128)(2,1)S(1)}, u32[]{:S(2)}, u32[]{:S(2)}) collective-permute-start(bf16[1040,512]{1,0:T(8,128)(2,1)} %copy-done.12), channel_id=1, source_target_pairs={{0,8},{8,0},{16,24},{24,16},{1,9},{9,1},{17,25},{25,17},{2,10},{10... | collective-permute-start | bytes 3194888 | tf_op jit(solution)/shard_map/ppermute | solution.py:26
  278.6 1.2 copy-start.9
  279.8 1.0 copy-start.11
  304.2 31.8 %collective-permute-start.42 = (bf16[528,256]{1,0:T(8,128)(2,1)S(1)}, bf16[528,256]{1,0:T(8,128)(2,1)S(1)}, u32[]{:S(2)}, u32[]{:S(2)}) collective-permute-start(bf16[528,256]{1,0:T(8,128)(2,1)S(1)} %get-tuple-element.160), channel_id=1, source_target_pairs={{0,8},{8,0},{16,24},{24,16},{1,9},{9,1},{17,25},{25,17},{2,10},{10... | collective-permute-start | bytes 811016 | tf_op jit(solution)/shard_map/ppermute | solution.py:26
  304.8 29.6 %collective-permute-start.44 = (bf16[528,256]{1,0:T(8,128)(2,1)S(1)}, bf16[528,256]{1,0:T(8,128)(2,1)S(1)}, u32[]{:S(2)}, u32[]{:S(2)}) collective-permute-start(bf16[528,256]{1,0:T(8,128)(2,1)S(1)} %get-tuple-element.167), channel_id=1, source_target_pairs={{0,16},{8,24},{16,0},{24,8},{1,17},{9,25},{17,1},{25,9},{2,18},{10... | collective-permute-start | bytes 811016 | tf_op jit(solution)/shard_map/ppermute | solution.py:26
  325.5 17.4 %collective-permute-start.36 = (bf16[528,512]{1,0:T(8,128)(2,1)S(1)}, bf16[528,512]{1,0:T(8,128)(2,1)S(1)}, u32[]{:S(2)}, u32[]{:S(2)}) collective-permute-start(bf16[528,512]{1,0:T(8,128)(2,1)S(1)} %get-tuple-element.147), channel_id=1, source_target_pairs={{0,16},{8,24},{16,0},{24,8},{1,17},{9,25},{17,1},{25,9},{2,18},{10... | collective-permute-start | bytes 1622024 | tf_op jit(solution)/shard_map/ppermute | solution.py:26
  327.0 17.4 %collective-permute-start.34 = (bf16[528,512]{1,0:T(8,128)(2,1)S(1)}, bf16[528,512]{1,0:T(8,128)(2,1)S(1)}, u32[]{:S(2)}, u32[]{:S(2)}) collective-permute-start(bf16[528,512]{1,0:T(8,128)(2,1)S(1)} %get-tuple-element.140), channel_id=1, source_target_pairs={{0,8},{8,0},{16,24},{24,16},{1,9},{9,1},{17,25},{25,17},{2,10},{10... | collective-permute-start | bytes 1622024 | tf_op jit(solution)/shard_map/ppermute | solution.py:26
  334.5 25.8 %collective-permute-start.45 = (bf16[528,768]{1,0:T(8,128)(2,1)S(1)}, bf16[528,768]{1,0:T(8,128)(2,1)S(1)}, u32[]{:S(2)}, u32[]{:S(2)}) collective-permute-start(bf16[528,768]{1,0:T(8,128)(2,1)S(1)} %get-tuple-element.168), channel_id=1, source_target_pairs={{0,16},{8,24},{16,0},{24,8},{1,17},{9,25},{17,1},{25,9},{2,18},{10... | collective-permute-start | bytes 2433032 | tf_op jit(solution)/shard_map/ppermute | solution.py:26
  336.1 26.1 %collective-permute-start.43 = (bf16[528,768]{1,0:T(8,128)(2,1)S(1)}, bf16[528,768]{1,0:T(8,128)(2,1)S(1)}, u32[]{:S(2)}, u32[]{:S(2)}) collective-permute-start(bf16[528,768]{1,0:T(8,128)(2,1)S(1)} %get-tuple-element.161), channel_id=1, source_target_pairs={{0,8},{8,0},{16,24},{24,16},{1,9},{9,1},{17,25},{25,17},{2,10},{10... | collective-permute-start | bytes 2433032 | tf_op jit(solution)/shard_map/ppermute | solution.py:26
  342.9 25.5 %collective-permute-start.37 = (bf16[528,512]{1,0:T(8,128)(2,1)S(1)}, bf16[528,512]{1,0:T(8,128)(2,1)S(1)}, u32[]{:S(2)}, u32[]{:S(2)}) collective-permute-start(bf16[528,512]{1,0:T(8,128)(2,1)S(1)} %get-tuple-element.148), channel_id=1, source_target_pairs={{0,16},{8,24},{16,0},{24,8},{1,17},{9,25},{17,1},{25,9},{2,18},{10... | collective-permute-start | bytes 1622024 | tf_op jit(solution)/shard_map/ppermute | solution.py:26
  344.4 25.2 %collective-permute-start.35 = (bf16[528,512]{1,0:T(8,128)(2,1)S(1)}, bf16[528,512]{1,0:T(8,128)(2,1)S(1)}, u32[]{:S(2)}, u32[]{:S(2)}) collective-permute-start(bf16[528,512]{1,0:T(8,128)(2,1)S(1)} %get-tuple-element.141), channel_id=1, source_target_pairs={{0,8},{8,0},{16,24},{24,16},{1,9},{9,1},{17,25},{25,17},{2,10},{10... | collective-permute-start | bytes 1622024 | tf_op jit(solution)/shard_map/ppermute | solution.py:26
  (1 other events, 0.8 us)
Sparse Core Ops, SparseCore 0:
  61.2 48.6 all-gather.4
  111.5 45.8 all-gather.6
